TPU v7x, 1024 devices: a whole 8x8x8 slice. The times are simulated.
1024 devices in a mesh: outer: 8 (over y_hi, core), inner: 128 (over z, y_lo, x).
Axes of the slice: x: 8, y: 8 (y_hi: 4, y_lo: 2; y = y_hi * 2 + y_lo), z: 8, core: 2. Of those that a mesh axis runs over, the one named last changes fastest.
Arguments:
- tok_mant: bfloat16 [256, 16384], P('inner', 'outer'), may hold values from -6 to 6
- tok_expo: int32 [256, 512], P('inner', 'outer'), may hold values from -3 to 1
- gate_mant: bfloat16 [16384, 53248], P('outer', 'inner'), may hold values from -0.046875 to 0.046875
- gate_expo: int32 [512, 53248], P('outer', 'inner'), may hold values from -3 to 1
- up_mant: bfloat16 [16384, 53248], P('outer', 'inner'), may hold values from -0.046875 to 0.046875
- up_expo: int32 [512, 53248], P('outer', 'inner'), may hold values from -3 to 1
Outputs:
- hidden: bfloat16 [256, 53248], P('outer', 'inner')
All inputs are finite; a program needn't handle non-finite values.
Results may differ from a plain program's by a relative error of at most 0.0017.
Values may be sent and summed in bfloat16 or wider, within the bound.
No kernel may reach another device: no remote copies, remote signals or barrier semaphores. Data moves between devices by JAX's collectives and lax.ppermute only.
A program may use at most 32 MiB of HBM per device.

v0:
```python
import jax
import jax.numpy as jnp
from jax import lax
from jax.sharding import PartitionSpec as P


def scaled_rows(mant, expo):
    rows, width = mant.shape
    factor = jnp.exp2(expo.astype(jnp.float32))
    return (
        (mant.astype(jnp.float32).reshape(rows, width // 32, 32) * factor[:, :, None])
        .reshape(rows, width)
        .astype(jnp.bfloat16)
    )


def scaled_columns(mant, expo):
    depth, width = mant.shape
    factor = jnp.exp2(expo.astype(jnp.float32))
    return (
        (mant.astype(jnp.float32).reshape(depth // 32, 32, width) * factor[:, None, :])
        .reshape(depth, width)
        .astype(jnp.bfloat16)
    )


def local(tok_mant, tok_expo, gate_mant, gate_expo, up_mant, up_expo):
    tokens = scaled_rows(tok_mant, tok_expo)
    weights = jnp.concatenate(
        (scaled_columns(gate_mant, gate_expo), scaled_columns(up_mant, up_expo)), axis=1
    )
    half = gate_mant.shape[1]
    terms = jnp.dot(
        lax.all_gather(tokens, "inner", axis=0, tiled=True),
        weights,
        preferred_element_type=jnp.float32,
    )
    summed = lax.psum_scatter(terms, "outer", scatter_dimension=0, tiled=True)
    gate = summed[:, :half]
    upper = summed[:, half:]
    return (jax.nn.silu(gate) * upper).astype(jnp.bfloat16)


def solution(mesh):
    placed = (
        P("inner", "outer"),
        P("inner", "outer"),
        P("outer", "inner"),
        P("outer", "inner"),
        P("outer", "inner"),
        P("outer", "inner"),
    )
    return jax.shard_map(
        local, mesh=mesh, in_specs=placed, out_specs=P("outer", "inner"), check_vma=False
    )
```

profile of v0, /device:TPU:1, one launch (start us, length us, event | category | flops | bytes accessed | tf_op | source)
XLA Modules:
  0.0 656.4 jit_solution(3357995000752321760)
XLA Ops:
  6.5 0.0 all-gather.3.cloned.1.call-start
  6.5 0.7 multiply_exponential_fusion.2
  7.2 0.1 mul.40
  7.3 0.1 mul.41
  7.4 1.3 fusion.7
  8.7 0.0 all-gather.3.cloned.1.call-update
  8.7 0.0 reduce-scatter.2.cloned.1.call-start
  8.8 2.8 copy.11
  11.6 0.0 copy-start.1
  11.6 0.0 copy-start.2
  11.6 3.8 copy.12
  15.4 0.0 copy-done.1
  15.5 0.0 copy-done.2
  15.5 4.5 fusion
  20.0 0.0 copy-start
  20.0 496.3 %all-gather.3.cloned.1.call-done = bf16[128,2,2048]{2,1,0:T(2,128)(2,1)} async-done(((bf16[1,2,2048]{2,1,0:T(2,128)(2,1)}), bf16[128,2,2048]{2,1,0:T(2,128)(2,1)}) %all-gather.3.cloned.1.call-update) | async-done | bytes 1048592 | tf_op jit(solution)/shard_map/all_gather | solution.py:34
  516.3 1.5 reshape.13
  517.8 0.0 copy-done
  517.8 3.9 fusion.2
  521.7 0.0 reduce-scatter.2.cloned.1.call-update
  521.7 126.3 %reduce-scatter.2.cloned.1.call-done = f32[32,832]{1,0:T(8,128)} async-done(((f32[256,832]{1,0:T(8,128)}), f32[32,832]{1,0:T(8,128)}) %reduce-scatter.2.cloned.1.call-update) | async-done | bytes 106512 | tf_op jit(solution)/shard_map/reduce_scatter | solution.py:38
  648.0 1.6 fusion.6
  (2 shorter events, 0.1 us)
Async XLA Ops:
  6.5 509.8 %all-gather.3.cloned.1.call-start = ((), (), s32[]{:S(2)}) async-start(), calls=%async_computation.2 | async-start | bytes 1056768 | tf_op jit(solution)/shard_map/all_gather | solution.py:34
  8.7 639.2 %reduce-scatter.2.cloned.1.call-start = ((), (), s32[]{:S(2)}) async-start(), calls=%async_computation.1 | async-start | bytes 1032192 | tf_op jit(solution)/shard_map/reduce_scatter | solution.py:38
  11.6 3.9 copy-start.1
  11.6 3.9 copy-start.2
  20.0 497.8 %copy-start = (bf16[2048,416]{1,0:T(8,128)(2,1)S(1)}, bf16[2048,416]{1,0:T(8,128)(2,1)}, u32[]{:S(2)}) copy-start(bf16[2048,416]{1,0:T(8,128)(2,1)} %get-tuple-element.5) | copy-start | bytes 5111812
Sparse Core Ops, SparseCore 0:
  10.0 506.2 all-gather.2
  521.8 126.0 reduce-scatter.1
where the time goes:
time: 657 us; the launch traced here: 656 us
  waiting for transfers between devices  623 us (95%)
  between operations  13.5 us (2%)
  local copies, waits for them, and re-layouts  8.26 us (1%)
  other arithmetic  8.12 us (1%)
    all_gather x1, waiting for transfers between devices, local(): lax.all_gather(tokens, 'inner', axis=0, tiled=True)  496 us
    reduce_scatter x1, waiting for transfers between devices, local(): summed = lax.psum_scatter(terms, 'outer', scatter_dimension=0, tiled=True)  126 us
  transfers between devices with their start and end apart: 2, of which 2 were waited for; matrix products, arithmetic and copies ran while one was open for 2% of the time, Pallas kernels for 0%

commit v1 on v0

v1 whole, which is shorter than its diff:
```python
import jax
import jax.numpy as jnp
from jax import lax
from jax.sharding import Mesh
from jax.sharding import PartitionSpec as P

AXES = ("yh", "c", "z", "yl", "x")
SIZES = (4, 2, 8, 2, 8)
OUTER = ("yh", "c")
INNER = ("z", "yl", "x")


def scaled_rows(mant, expo):
    rows, width = mant.shape
    factor = jnp.exp2(expo.astype(jnp.float32))
    return (
        (mant.astype(jnp.float32).reshape(rows, width // 32, 32) * factor[:, :, None])
        .reshape(rows, width)
        .astype(jnp.bfloat16)
    )


def scaled_columns(mant, expo):
    depth, width = mant.shape
    factor = jnp.exp2(expo.astype(jnp.float32))
    return (
        (mant.astype(jnp.float32).reshape(depth // 32, 32, width) * factor[:, None, :])
        .reshape(depth, width)
        .astype(jnp.bfloat16)
    )


def gathered(block, axes, count):
    copies = jnp.broadcast_to(block[None], (count,) + block.shape)
    return lax.all_to_all(copies, axes, 0, 0)


def summed_shares(terms):
    width = terms.shape[1]
    parts = terms.reshape(4, 2, 32, width)
    core, row = lax.axis_index("c"), lax.axis_index("yh")
    own = lax.dynamic_index_in_dim(parts, core, 1, False)
    other = lax.dynamic_index_in_dim(parts, 1 - core, 1, False)
    pair = own + lax.ppermute(other, "c", [(0, 1), (1, 0)])
    total = lax.dynamic_index_in_dim(pair, row, 0, False)
    for step in (2, 1, 3):
        ahead = lax.dynamic_index_in_dim(pair, (row + step) % 4, 0, False)
        total = total + lax.ppermute(ahead, "yh", [(i, (i + step) % 4) for i in range(4)])
    return total


def local(tok_mant, tok_expo, gate_mant, gate_expo, up_mant, up_expo):
    tokens = scaled_rows(tok_mant, tok_expo)
    weights = jnp.concatenate(
        (scaled_columns(gate_mant, gate_expo), scaled_columns(up_mant, up_expo)), axis=1
    )
    half = gate_mant.shape[1]
    everyone = gathered(tokens, INNER, 128).reshape(256, tokens.shape[1])
    terms = jnp.dot(everyone, weights, preferred_element_type=jnp.float32)
    summed = summed_shares(terms)
    return (jax.nn.silu(summed[:, :half]) * summed[:, half:]).astype(jnp.bfloat16)


def solution(mesh):
    fine = Mesh(mesh.devices.reshape(SIZES), AXES)
    placed = (
        P(INNER, OUTER),
        P(INNER, OUTER),
        P(OUTER, INNER),
        P(OUTER, INNER),
        P(OUTER, INNER),
        P(OUTER, INNER),
    )
    return jax.shard_map(
        local, mesh=fine, in_specs=placed, out_specs=P(OUTER, INNER), check_vma=False
    )
```

time: 657 us -> 89.3 us (0.14)
  waiting for transfers between devices: 623 us -> 15.1 us
  starting transfers between devices: 0.04 us -> 44.7 us
  between operations: 13.5 us -> 0.19 us
  local copies, waits for them, and re-layouts: 8.26 us -> 17.3 us
    all_gather x1 -> x0, waiting for transfers between devices: 496 us -> none  [local(): lax.all_gather(tokens, 'inner', axis=0, tiled=True)]
    reduce_scatter x1 -> x0, waiting for transfers between devices: 126 us -> none  [local(): summed = lax.psum_scatter(terms, 'outer', scatter_dimension=0, tiled=True)]
    all_to_all x0 -> x1, starting transfers between devices: none -> 26 us  [gathered(): return lax.all_to_all(copies, axes, 0, 0)]
    ppermute x0 -> x4, starting transfers between devices: none -> 18.7 us  [the longest x3 14.4 us: summed_shares(): lax.ppermute(ahead, 'yh', [(i, (i + step) % 4) for i in range(4)])]
    mul x0 -> x4, local copies, waits for them, and re-layouts: none -> 14 us  [scaled_columns(): mant.astype(jnp.float32).reshape(depth // 32, 32, width)]
    all_to_all x0 -> x1, waiting for transfers between devices: none -> 8.83 us  [gathered(): return lax.all_to_all(copies, axes, 0, 0)]
    unnamed x9 -> x4, local copies, waits for them, and re-layouts: 8.08 us -> 0.01 us
  transfers between devices with their start and end apart: 2 -> 5, of which waited for: 2 -> 4; matrix products, arithmetic and copies ran while one was open for 2% -> 23% of each run, Pallas kernels for 0% -> 0%
where the time goes in v1:
time: 89.3 us; the launch traced here: 88.8 us
  starting transfers between devices  44.7 us (50%)
  local copies, waits for them, and re-layouts  17.3 us (19%)
  waiting for transfers between devices  15.1 us (17%)
  other arithmetic  8.26 us (9%)
  matrix products  3.24 us (4%)
    all_to_all x1, starting transfers between devices, gathered(): return lax.all_to_all(copies, axes, 0, 0)  26 us
    ppermute x3, starting transfers between devices, summed_shares(): lax.ppermute(ahead, 'yh', [(i, (i + step) % 4) for i in range(4)])  14.4 us
    mul x4, local copies, waits for them, and re-layouts, scaled_columns(): mant.astype(jnp.float32).reshape(depth // 32, 32, width)  14 us
    all_to_all x1, waiting for transfers between devices, gathered(): return lax.all_to_all(copies, axes, 0, 0)  8.83 us
    convert_element_type x1, other arithmetic, scaled_columns(): return (mant.astype(jnp.float32).reshape(depth // 32, 32, width) * factor...  6 us
    ppermute x3, waiting for transfers between devices, summed_shares(): lax.ppermute(ahead, 'yh', [(i, (i + step) % 4) for i in range(4)])  4.89 us
    ppermute x1, starting transfers between devices, summed_shares(): pair = own + lax.ppermute(other, 'c', [(0, 1), (1, 0)])  4.25 us
    dot_general x1, matrix products, local(): terms = jnp.dot(everyone, weights, preferred_element_type=jnp.float32)  3.24 us
  transfers between devices with their start and end apart: 5, of which 4 were waited for; matrix products, arithmetic and copies ran while one was open for 23% of the time, Pallas kernels for 0%

profile of v1, /device:TPU:1, one launch (start us, length us, event | category | flops | bytes accessed | tf_op | source)
XLA Modules:
  0.0 88.8 jit_solution(3281609173558144476)
XLA Ops:
  0.0 0.0 copy-start
  0.0 0.7 multiply_exponential_fusion.2
  0.7 0.1 mul.40
  0.8 0.1 mul.41
  0.9 0.7 multiply_convert_fusion.2
  1.6 1.6 %broadcast_in_dim.2 = bf16[128,2,2048]{2,1,0:T(2,128)(2,1)} broadcast(bf16[2,2048]{1,0:T(2,128)(2,1)S(1)} %multiply_convert_fusion.2), dimensions={1,2} | broadcast | bytes 1056768 | tf_op jit(solution)/shard_map/broadcast_in_dim | solution.py:34
  3.2 26.0 %all-to-all-start = ((bf16[128,2,2048]{2,1,0:T(2,128)(2,1)}), bf16[128,2,2048]{2,1,0:T(2,128)(2,1)}, u32[]{:S(2)}, u32[]{:S(2)}) async-start(bf16[128,2,2048]{2,1,0:T(2,128)(2,1)} %broadcast_in_dim.2), calls=%async_computation | async-start | bytes 2097152 | tf_op jit(solution)/shard_map/all_to_all | solution.py:35
  29.3 0.0 copy-done
  29.3 2.5 %mul.46 = f32[64,32,416]{2,1,0:T(8,128)} broadcast(f32[64,416]{1,0:T(8,128)S(1)} %multiply_exponential_fusion), dimensions={0,2} | broadcast | bytes 3514368 | tf_op jit(solution)/shard_map/mul | solution.py:27
  31.8 0.0 copy-start.1
  31.8 3.8 %copy.10 = f32[2048,416]{0,1:T(8,128)S(1)} copy(f32[2048,416]{1,0:T(8,128)} %bitcast.24) | data formatting | bytes 6815744 | tf_op jit(solution)/shard_map/mul | solution.py:27
  35.6 0.0 copy-done.1
  35.7 2.5 %mul.43 = f32[64,32,416]{2,1,0:T(8,128)} broadcast(f32[64,416]{1,0:T(8,128)S(1)} %multiply_exponential_fusion.1), dimensions={0,2} | broadcast | bytes 3514368 | tf_op jit(solution)/shard_map/mul | solution.py:27
  38.1 5.2 %copy.9 = f32[2048,416]{0,1:T(8,128)} copy(f32[2048,416]{1,0:T(8,128)} %bitcast.25) | data formatting | bytes 6815744 | tf_op jit(solution)/shard_map/mul | solution.py:27
  43.4 6.0 %multiply_convert_fusion = (bf16[2048,416]{0,1:T(8,128)(2,1)}, bf16[2048,416]{0,1:T(8,128)(2,1)}) fusion(f32[2048,416]{0,1:T(8,128)S(1)} %copy.10, bf16[2048,416]{0,1:T(8,128)(2,1)} %param.10, f32[2048,416]{0,1:T(8,128)} %copy.9, bf16[2048,416]{0,1:T(8,128)(2,1)} %param.8), kind=kLoop, calls=%fused_computation.4 | loop fusion | flops 5111808 | bytes 13631488 | tf_op jit(solution)/shard_map/convert_element_type | solution.py:29
  49.4 8.8 %all-to-all-done = bf16[128,2,2048]{2,1,0:T(2,128)(2,1)} async-done(((bf16[128,2,2048]{2,1,0:T(2,128)(2,1)}), bf16[128,2,2048]{2,1,0:T(2,128)(2,1)}, u32[]{:S(2)}, u32[]{:S(2)}) %all-to-all-start) | async-done | bytes 1048608 | tf_op jit(solution)/shard_map/all_to_all | solution.py:35
  58.2 1.5 %dot_general.5 = bf16[4,2,32,2048]{3,2,1,0:T(8,128)(2,1)S(1)} reshape(bf16[128,2,2048]{2,1,0:T(2,128)(2,1)} %all-to-all-done) | data formatting | bytes 2097152 | tf_op jit(solution)/shard_map/dot_general | solution.py:59
  59.7 3.2 %fusion = f32[4,2,32,832]{3,2,1,0:T(8,128)S(1)} fusion(bf16[4,2,32,2048]{3,2,1,0:T(8,128)(2,1)S(1)} %dot_general.5, bf16[2048,416]{0,1:T(8,128)(2,1)} %get-tuple-element.8, bf16[2048,416]{0,1:T(8,128)(2,1)} %get-tuple-element.9), kind=kOutput, calls=%fused_computation.1 | convolution fusion | flops 879230976 | bytes 5308416 | tf_op jit(solution)/shard_map/dot_general | solution.py:59
  63.0 4.2 %collective-permute-start = (f32[4,32,832]{2,1,0:T(8,128)S(1)}, f32[4,32,832]{2,1,0:T(8,128)S(1)}, u32[]{:S(2)}, u32[]{:S(2)}) collective-permute-start(f32[4,32,832]{2,1,0:T(8,128)S(1)} %dynamic-slice_bitcast_fusion), channel_id=1, source_target_pairs={{0,128},{128,0},{1,129},{129,1},{2,130},{130,2},{3,131},{131,3},{4... | collective-permute-start | bytes 1277960 | tf_op jit(solution)/shard_map/ppermute | solution.py:44
  67.3 1.4 %collective-permute-done = f32[4,32,832]{2,1,0:T(8,128)S(1)} collective-permute-done((f32[4,32,832]{2,1,0:T(8,128)S(1)}, f32[4,32,832]{2,1,0:T(8,128)S(1)}, u32[]{:S(2)}, u32[]{:S(2)}) %collective-permute-start) | collective-permute-done | bytes 426016 | tf_op jit(solution)/shard_map/ppermute | solution.py:44
  68.6 0.1 bitcast_add_fusion
  68.7 7.0 %collective-permute-start.1 = (f32[32,832]{1,0:T(8,128)S(1)}, f32[32,832]{1,0:T(8,128)S(1)}, u32[]{:S(2)}, u32[]{:S(2)}) collective-permute-start(f32[32,832]{1,0:T(8,128)S(1)} %get-tuple-element.5), channel_id=1, source_target_pairs={{0,512},{256,768},{512,0},{768,256},{1,513},{257,769},{513,1},{769... | collective-permute-start | bytes 319496 | tf_op jit(solution)/shard_map/ppermute | solution.py:48
  75.8 2.6 %collective-permute-start.2 = (f32[32,832]{1,0:T(8,128)S(1)}, f32[32,832]{1,0:T(8,128)S(1)}, u32[]{:S(2)}, u32[]{:S(2)}) collective-permute-start(f32[32,832]{1,0:T(8,128)S(1)} %get-tuple-element.7), channel_id=1, source_target_pairs={{0,256},{256,512},{512,768},{768,0},{1,257},{257,513},{513,769},{7... | collective-permute-start | bytes 319496 | tf_op jit(solution)/shard_map/ppermute | solution.py:48
  78.4 4.7 %collective-permute-start.3 = (f32[32,832]{1,0:T(8,128)S(1)}, f32[32,832]{1,0:T(8,128)S(1)}, u32[]{:S(2)}, u32[]{:S(2)}) collective-permute-start(f32[32,832]{1,0:T(8,128)S(1)} %get-tuple-element.6), channel_id=1, source_target_pairs={{0,768},{256,0},{512,256},{768,512},{1,769},{257,1},{513,257},{769... | collective-permute-start | bytes 319496 | tf_op jit(solution)/shard_map/ppermute | solution.py:48
  83.2 0.0 collective-permute-done.1
  83.2 1.2 %collective-permute-done.2 = f32[32,832]{1,0:T(8,128)S(1)} collective-permute-done((f32[32,832]{1,0:T(8,128)S(1)}, f32[32,832]{1,0:T(8,128)S(1)}, u32[]{:S(2)}, u32[]{:S(2)}) %collective-permute-start.2) | collective-permute-done | bytes 106528 | tf_op jit(solution)/shard_map/ppermute | solution.py:48
  84.4 3.7 %collective-permute-done.3 = f32[32,832]{1,0:T(8,128)S(1)} collective-permute-done((f32[32,832]{1,0:T(8,128)S(1)}, f32[32,832]{1,0:T(8,128)S(1)}, u32[]{:S(2)}, u32[]{:S(2)}) %collective-permute-start.3) | collective-permute-done | bytes 106528 | tf_op jit(solution)/shard_map/ppermute | solution.py:48
  88.1 0.7 fusion.5
  (5 shorter events, 0.2 us)
Async XLA Ops:
  0.0 29.3 %copy-start = (s32[64,416]{1,0:T(8,128)S(1)}, s32[64,416]{1,0:T(8,128)}, u32[]{:S(2)}) copy-start(s32[64,416]{1,0:T(8,128)} %param.11) | copy-start | bytes 319492
  3.2 55.0 %all-to-all-start = ((bf16[128,2,2048]{2,1,0:T(2,128)(2,1)}), bf16[128,2,2048]{2,1,0:T(2,128)(2,1)}, u32[]{:S(2)}, u32[]{:S(2)}) async-start(bf16[128,2,2048]{2,1,0:T(2,128)(2,1)} %broadcast_in_dim.2), calls=%async_computation | async-start | bytes 2097152 | tf_op jit(solution)/shard_map/all_to_all | solution.py:35
  31.8 3.8 %copy-start.1 = (s32[64,416]{1,0:T(8,128)S(1)}, s32[64,416]{1,0:T(8,128)}, u32[]{:S(2)}) copy-start(s32[64,416]{1,0:T(8,128)} %param.9) | copy-start | bytes 319492
  63.0 5.7 %collective-permute-start = (f32[4,32,832]{2,1,0:T(8,128)S(1)}, f32[4,32,832]{2,1,0:T(8,128)S(1)}, u32[]{:S(2)}, u32[]{:S(2)}) collective-permute-start(f32[4,32,832]{2,1,0:T(8,128)S(1)} %dynamic-slice_bitcast_fusion), channel_id=1, source_target_pairs={{0,128},{128,0},{1,129},{129,1},{2,130},{130,2},{3,131},{131,3},{4... | collective-permute-start | bytes 1277960 | tf_op jit(solution)/shard_map/ppermute | solution.py:44
  68.7 14.4 %collective-permute-start.1 = (f32[32,832]{1,0:T(8,128)S(1)}, f32[32,832]{1,0:T(8,128)S(1)}, u32[]{:S(2)}, u32[]{:S(2)}) collective-permute-start(f32[32,832]{1,0:T(8,128)S(1)} %get-tuple-element.5), channel_id=1, source_target_pairs={{0,512},{256,768},{512,0},{768,256},{1,513},{257,769},{513,1},{769... | collective-permute-start | bytes 319496 | tf_op jit(solution)/shard_map/ppermute | solution.py:48
  75.8 8.6 %collective-permute-start.2 = (f32[32,832]{1,0:T(8,128)S(1)}, f32[32,832]{1,0:T(8,128)S(1)}, u32[]{:S(2)}, u32[]{:S(2)}) collective-permute-start(f32[32,832]{1,0:T(8,128)S(1)} %get-tuple-element.7), channel_id=1, source_target_pairs={{0,256},{256,512},{512,768},{768,0},{1,257},{257,513},{513,769},{7... | collective-permute-start | bytes 319496 | tf_op jit(solution)/shard_map/ppermute | solution.py:48
  78.4 9.7 %collective-permute-start.3 = (f32[32,832]{1,0:T(8,128)S(1)}, f32[32,832]{1,0:T(8,128)S(1)}, u32[]{:S(2)}, u32[]{:S(2)}) collective-permute-start(f32[32,832]{1,0:T(8,128)S(1)} %get-tuple-element.6), channel_id=1, source_target_pairs={{0,768},{256,0},{512,256},{768,512},{1,769},{257,1},{513,257},{769... | collective-permute-start | bytes 319496 | tf_op jit(solution)/shard_map/ppermute | solution.py:48

commit v2 on v1

v2 whole, which is shorter than its diff:
```python
import jax
import jax.numpy as jnp
from jax import lax
from jax.experimental import pallas as pl
from jax.experimental.pallas import tpu as pltpu
from jax.sharding import Mesh
from jax.sharding import PartitionSpec as P

AXES = ("yh", "c", "zh", "zl", "yl", "xh", "xl")
SIZES = (4, 2, 4, 2, 2, 4, 2)
OUTER = ("yh", "c")
INNER = ("zh", "zl", "yl", "xh", "xl")
FAR = ("zh", "xh")
NEAR = ("zl", "yl", "xl")


def copies_kernel(mant_ref, expo_ref, out_ref):
    blocks, width = expo_ref.shape[1], mant_ref.shape[1]
    group = lax.broadcasted_iota(jnp.int32, (blocks, width), 1) // (width // blocks)
    spread = (group == lax.broadcasted_iota(jnp.int32, (blocks, width), 0)).astype(jnp.bfloat16)
    factor = jnp.exp2(expo_ref[...].astype(jnp.float32)).astype(jnp.bfloat16)
    scale = jnp.dot(factor, spread, preferred_element_type=jnp.float32)
    scaled = (mant_ref[...].astype(jnp.float32) * scale).astype(jnp.bfloat16)
    out_ref[...] = jnp.broadcast_to(scaled[None], out_ref.shape)


def scaled_copies(mant, expo, count):
    return pl.pallas_call(
        copies_kernel,
        out_shape=jax.ShapeDtypeStruct((count,) + mant.shape, jnp.bfloat16),
        compiler_params=pltpu.CompilerParams(vmem_limit_bytes=56 << 20),
    )(mant, expo)


def weights_kernel(gate_ref, gate_expo_ref, up_ref, up_expo_ref, out_ref):
    def scaled(mant_ref, expo_ref):
        factor = jnp.exp2(expo_ref[...].astype(jnp.float32)).astype(jnp.bfloat16)
        scale = lax.dot_general(
            factor, spread, (((0,), (0,)), ((), ())), preferred_element_type=jnp.float32
        )
        return (mant_ref[...].astype(jnp.float32) * scale).astype(jnp.bfloat16)

    blocks, half, width = gate_expo_ref.shape[0], gate_ref.shape[0], gate_ref.shape[1]
    first = pl.program_id(0) * width
    block = (first + lax.broadcasted_iota(jnp.int32, (blocks, width), 1)) // 32
    spread = (block == lax.broadcasted_iota(jnp.int32, (blocks, width), 0)).astype(jnp.bfloat16)
    out_ref[:half] = scaled(gate_ref, gate_expo_ref)
    out_ref[half:] = scaled(up_ref, up_expo_ref)


def scaled_weights(gate_mant, gate_expo, up_mant, up_expo):
    depth, half = gate_mant.shape
    steps = 4
    mant = pl.BlockSpec((half, depth // steps), lambda i: (0, i))
    expo = pl.BlockSpec(gate_expo.shape, lambda i: (0, 0))
    return pl.pallas_call(
        weights_kernel,
        grid=(steps,),
        in_specs=[mant, expo, mant, expo],
        out_specs=pl.BlockSpec((2 * half, depth // steps), lambda i: (0, i)),
        out_shape=jax.ShapeDtypeStruct((2 * half, depth), jnp.bfloat16),
        compiler_params=pltpu.CompilerParams(vmem_limit_bytes=24 << 20),
        cost_estimate=pl.CostEstimate(
            flops=4 * half * depth * 64, bytes_accessed=8 * half * depth, transcendentals=0
        ),
    )(gate_mant.T, gate_expo, up_mant.T, up_expo)


def product_kernel(side_ref, rows_ref, weights_ref, out_ref):
    width = rows_ref.shape[-1]
    rows = jnp.transpose(rows_ref[0], (2, 0, 3, 1, 4, 5)).reshape(-1, width)
    out_ref[...] = lax.dot_general(
        rows, weights_ref[...], (((1,), (1,)), ((), ())), preferred_element_type=jnp.float32
    )


def product(side, everyone, weights):
    count, units = everyone.size // everyone.shape[-1] // 2, weights.shape[0]
    return pl.pallas_call(
        product_kernel,
        grid_spec=pltpu.PrefetchScalarGridSpec(
            num_scalar_prefetch=1,
            grid=(1,),
            in_specs=[
                pl.BlockSpec((1,) + everyone.shape[1:], lambda i, side: (side[0],) + (0,) * 6),
                pl.BlockSpec(weights.shape, lambda i, side: (0, 0)),
            ],
            out_specs=pl.BlockSpec((count, units), lambda i, side: (0, 0)),
        ),
        out_shape=jax.ShapeDtypeStruct((count, units), jnp.float32),
        compiler_params=pltpu.CompilerParams(vmem_limit_bytes=24 << 20),
        cost_estimate=pl.CostEstimate(
            flops=2 * count * weights.size, bytes_accessed=2 * weights.size, transcendentals=0
        ),
    )(side.reshape(1), everyone, weights)


def summed_shares(everyone, weights):
    core = lax.axis_index("c")
    theirs = lax.ppermute(product(1 - core, everyone, weights), "c", [(0, 1), (1, 0)])
    pair = product(core, everyone, weights) + theirs
    parts = lax.all_to_all(pair.reshape(4, 32, -1), "yh", 0, 0)
    return jnp.sum(parts, axis=0)


def gathered(tok_mant, tok_expo):
    far = lax.all_to_all(scaled_copies(tok_mant, tok_expo, 16), FAR, 0, 0)
    near = lax.all_to_all(jnp.broadcast_to(far[None], (8,) + far.shape), NEAR, 0, 0)
    return near.reshape((2, 2, 2, 4, 4) + tok_mant.shape)


def local(tok_mant, tok_expo, gate_mant, gate_expo, up_mant, up_expo):
    weights = scaled_weights(gate_mant, gate_expo, up_mant, up_expo)
    half = gate_mant.shape[1]
    everyone = gathered(tok_mant, tok_expo)
    summed = summed_shares(everyone, weights)
    return (jax.nn.silu(summed[:, :half]) * summed[:, half:]).astype(jnp.bfloat16)


def solution(mesh):
    fine = Mesh(mesh.devices.reshape(SIZES), AXES)
    placed = (
        P(INNER, OUTER),
        P(INNER, OUTER),
        P(OUTER, INNER),
        P(OUTER, INNER),
        P(OUTER, INNER),
        P(OUTER, INNER),
    )
    return jax.shard_map(
        local, mesh=fine, in_specs=placed, out_specs=P(OUTER, INNER), check_vma=False
    )
```

time: 89.3 us -> 85.6 us (0.959)
  blocking collectives: 0 us -> 53.4 us
  starting transfers between devices: 44.7 us -> 9.68 us
  local copies, waits for them, and re-layouts: 17.3 us -> 5.54 us
  Pallas kernels: 0 us -> 8.36 us
  waiting for transfers between devices: 15.1 us -> 7.32 us
  other arithmetic: 8.26 us -> 0.78 us
  matrix products: 3.24 us -> 0 us
    all_to_all x0 -> x2, blocking collectives: none -> 53.4 us  [the longest x1 32.9 us: gathered(): far = lax.all_to_all(scaled_copies(tok_mant, tok_expo, 16), FAR, 0, 0)]
    all_to_all x1, starting transfers between devices: 26 us -> 4.5 us  [gathered(): lax.all_to_all(jnp.broadcast_to(far[None], (8,) + far.shape), NEAR, 0, 0)]
    mul x6 -> x0, local copies, waits for them, and re-layouts: 14.2 us -> none  [the longest x4 14 us: scaled_columns(): mant.astype(jnp.float32).reshape(depth // 32, 32, width)]
    ppermute x4 -> x1, starting transfers between devices: 18.7 us -> 5.17 us  [summed_shares(): lax.ppermute(product(1 - core, everyone, weights), 'c', [(0, 1), (1, 0)])]
    pallas_call x0 -> x4, Pallas kernels: none -> 8.36 us  [the longest x2 4.62 us: product(): pl.pallas_call(product_kernel, grid_spec=pltpu.PrefetchScalarGridSpec(num...]
    convert_element_type x2 -> x0, other arithmetic: 6.71 us -> none  [the longest x1 6 us: scaled_columns(): return (mant.astype(jnp.float32).reshape(depth // 32, 32, width) * factor...]
    ppermute x4 -> x1, waiting for transfers between devices: 6.27 us -> 0.01 us  [summed_shares(): lax.ppermute(product(1 - core, everyone, weights), 'c', [(0, 1), (1, 0)])]
    unnamed x4 -> x8, local copies, waits for them, and re-layouts: 0.01 us -> 3.81 us
  transfers between devices with their start and end apart: 5 -> 2, of which waited for: 4 -> 1; matrix products, arithmetic and copies ran while one was open for 23% -> 0% of each run, Pallas kernels for 0% -> 5%
where the time goes in v2:
time: 85.6 us; the launch traced here: 85.1 us
  blocking collectives  53.4 us (62%)
  starting transfers between devices  9.68 us (11%)
  Pallas kernels  8.36 us (10%)
  waiting for transfers between devices  7.32 us (9%)
  local copies, waits for them, and re-layouts  5.54 us (6%)
    all_to_all x1, blocking collectives, gathered(): far = lax.all_to_all(scaled_copies(tok_mant, tok_expo, 16), FAR, 0, 0)  32.9 us
    all_to_all x1, blocking collectives, summed_shares(): parts = lax.all_to_all(pair.reshape(4, 32, -1), 'yh', 0, 0)  20.5 us
    all_to_all x1, waiting for transfers between devices, gathered(): lax.all_to_all(jnp.broadcast_to(far[None], (8,) + far.shape), NEAR, 0, 0)  7.32 us
    ppermute x1, starting transfers between devices, summed_shares(): lax.ppermute(product(1 - core, everyone, weights), 'c', [(0, 1), (1, 0)])  5.17 us
    pallas_call x2, Pallas kernels, product(): pl.pallas_call(product_kernel, grid_spec=pltpu.PrefetchScalarGridSpec(num...  4.62 us
    all_to_all x1, starting transfers between devices, gathered(): lax.all_to_all(jnp.broadcast_to(far[None], (8,) + far.shape), NEAR, 0, 0)  4.5 us
    unnamed x8, local copies, waits for them, and re-layouts  3.81 us
    pallas_call x1, Pallas kernels, scaled_weights(): pl.pallas_call(weights_kernel, grid=(steps,), in_specs=[mant, expo, mant,...  2.21 us
  transfers between devices with their start and end apart: 2, of which 1 were waited for; matrix products, arithmetic and copies ran while one was open for 0% of the time, Pallas kernels for 5%

profile of v2, /device:TPU:1, one launch (start us, length us, event | category | flops | bytes accessed | tf_op | source)
XLA Modules:
  0.0 85.1 jit_solution(6070234161160384308)
XLA Ops:
  0.0 1.5 %shard_map.64 = bf16[16,2,2048]{2,1,0:T(2,128)(2,1)} custom-call(bf16[2,2048]{1,0:T(2,128)(2,1)} %mant_ref.1, s32[2,64]{1,0:T(2,128)} %expo_ref.1), custom_call_target="tpu_custom_call" | custom-call | tf_op jit(solution)/shard_map/pallas_call | solution.py:28
  1.5 32.9 %all_to_all.15 = bf16[16,2,2048]{2,1,0:T(2,128)(2,1)S(1)} all-to-all(bf16[16,2,2048]{2,1,0:T(2,128)(2,1)} %shard_map.64), channel_id=1, replica_groups=mesh['yh'=4,'c'=2,'zh'=4,'zl'=2,'yl'=2,'xh'=4,'xl'=2] {'zh','xh'}, dimensions={0} | all-to-all | bytes 262144 | tf_op jit(solution)/shard_map/all_to_all | solution.py:107
  34.4 0.0 copy-start.2
  34.4 1.7 %broadcast_in_dim.2 = bf16[8,16,2,2048]{3,2,1,0:T(2,128)(2,1)} broadcast(bf16[16,2,2048]{2,1,0:T(2,128)(2,1)S(1)} %all_to_all.15), dimensions={1,2,3} | broadcast | bytes 1179648 | tf_op jit(solution)/shard_map/broadcast_in_dim | solution.py:108
  36.1 4.5 %all-to-all-start.1 = ((bf16[8,16,2,2048]{3,2,1,0:T(2,128)(2,1)}), bf16[8,16,2,2048]{3,2,1,0:T(2,128)(2,1)}, u32[]{:S(2)}, u32[]{:S(2)}) async-start(bf16[8,16,2,2048]{3,2,1,0:T(2,128)(2,1)} %broadcast_in_dim.2), calls=%async_computation.1 | async-start | bytes 2097152 | tf_op jit(solution)/shard_map/all_to_all | solution.py:108
  40.6 0.0 copy-done.2
  40.6 0.0 copy-start
  40.6 1.4 %copy-done = bf16[2048,416]{0,1:T(8,128)(2,1)S(1)} copy-done((bf16[2048,416]{0,1:T(8,128)(2,1)S(1)}, bf16[2048,416]{0,1:T(8,128)(2,1)}, u32[]{:S(2)}) %copy-start) | copy-done | bytes 1703960
  42.1 0.0 copy-start.1
  42.1 1.5 %copy-done.1 = bf16[2048,416]{0,1:T(8,128)(2,1)S(1)} copy-done((bf16[2048,416]{0,1:T(8,128)(2,1)S(1)}, bf16[2048,416]{0,1:T(8,128)(2,1)}, u32[]{:S(2)}) %copy-start.1) | copy-done | bytes 1703960
  43.5 0.0 copy-start.3
  43.5 0.9 %copy-done.3 = s32[64,416]{1,0:T(8,128)S(1)} copy-done((s32[64,416]{1,0:T(8,128)S(1)}, s32[64,416]{1,0:T(8,128)}, u32[]{:S(2)}) %copy-start.3) | copy-done | bytes 106520
  44.4 2.2 %shard_map.65.weights_ref = bf16[832,2048]{1,0:T(8,128)(2,1)S(1)} custom-call(bf16[416,2048]{1,0:T(8,128)(2,1)S(1)} %bitcast.6, s32[64,416]{1,0:T(8,128)S(1)} %copy-done.2, bf16[416,2048]{1,0:T(8,128)(2,1)S(1)} %bitcast.7, s32[64,416]{1,0:T(8,128)S(1)} %copy-done.3), custom_call_target="tpu_custom_call" | custom-call | flops 218103808 | bytes 6815744 | tf_op jit(solution)/shard_map/pallas_call | solution.py:56
  46.7 7.3 %all-to-all-done.1 = bf16[8,16,2,2048]{3,2,1,0:T(2,128)(2,1)} async-done(((bf16[8,16,2,2048]{3,2,1,0:T(2,128)(2,1)}), bf16[8,16,2,2048]{3,2,1,0:T(2,128)(2,1)}, u32[]{:S(2)}, u32[]{:S(2)}) %all-to-all-start.1) | async-done | bytes 1048608 | tf_op jit(solution)/shard_map/all_to_all | solution.py:108
  54.0 2.3 %shard_map.67 = f32[128,832]{1,0:T(8,128)S(1)} custom-call(s32[1]{0:T(128)} %bitcast.4.side_ref, bf16[2,2,2,4,4,2,2048]{6,5,4,3,2,1,0:T(2,128)(2,1)} %bitcast.1.rows_ref, bf16[832,2048]{1,0:T(8,128)(2,1)S(1)} %shard_map.65.weights_ref), custom_call_target="tpu_custom_call" | custom-call | flops 436207616 | bytes 3407872 | tf_op jit(solution)/shard_map/pallas_call | solution.py:79
  56.3 5.2 %collective-permute-start = (f32[128,832]{1,0:T(8,128)S(1)}, f32[128,832]{1,0:T(8,128)S(1)}, u32[]{:S(2)}, u32[]{:S(2)}) collective-permute-start(f32[128,832]{1,0:T(8,128)S(1)} %shard_map.67), channel_id=1, source_target_pairs={{0,128},{128,0},{1,129},{129,1},{2,130},{130,2},{3,131},{131,3},{4... | collective-permute-start | bytes 1277960 | tf_op jit(solution)/shard_map/ppermute | solution.py:100
  61.5 2.3 %shard_map.66 = f32[128,832]{1,0:T(8,128)S(1)} custom-call(s32[1]{0:T(128)} %bitcast.side_ref, bf16[2,2,2,4,4,2,2048]{6,5,4,3,2,1,0:T(2,128)(2,1)} %bitcast.1.rows_ref, bf16[832,2048]{1,0:T(8,128)(2,1)S(1)} %shard_map.65.weights_ref), custom_call_target="tpu_custom_call" | custom-call | flops 436207616 | bytes 3407872 | tf_op jit(solution)/shard_map/pallas_call | solution.py:79
  63.8 0.0 collective-permute-done
  63.8 0.1 add.7
  63.9 20.5 %all_to_all.16 = f32[4,32,832]{2,1,0:T(8,128)S(1)} all-to-all(f32[4,32,832]{2,1,0:T(8,128)S(1)} %bitcast.8), channel_id=1, replica_groups=mesh['yh'=4,'c'=2,'zh'=4,'zl'=2,'yl'=2,'xh'=4,'xl'=2] {'yh'}, dimensions={0} | all-to-all | bytes 851968 | tf_op jit(solution)/shard_map/all_to_all | solution.py:102
  84.4 0.7 fusion
  (1 shorter events, 0.0 us)
Async XLA Ops:
  34.4 6.2 %copy-start.2 = (s32[64,416]{1,0:T(8,128)S(1)}, s32[64,416]{1,0:T(8,128)}, u32[]{:S(2)}) copy-start(s32[64,416]{1,0:T(8,128)} %gate_expo_ref.1) | copy-start | bytes 319492
  36.1 17.9 %all-to-all-start.1 = ((bf16[8,16,2,2048]{3,2,1,0:T(2,128)(2,1)}), bf16[8,16,2,2048]{3,2,1,0:T(2,128)(2,1)}, u32[]{:S(2)}, u32[]{:S(2)}) async-start(bf16[8,16,2,2048]{3,2,1,0:T(2,128)(2,1)} %broadcast_in_dim.2), calls=%async_computation.1 | async-start | bytes 2097152 | tf_op jit(solution)/shard_map/all_to_all | solution.py:108
  40.6 1.5 %copy-start = (bf16[2048,416]{0,1:T(8,128)(2,1)S(1)}, bf16[2048,416]{0,1:T(8,128)(2,1)}, u32[]{:S(2)}) copy-start(bf16[2048,416]{0,1:T(8,128)(2,1)} %param.8) | copy-start | bytes 5111812
  42.1 1.5 %copy-start.1 = (bf16[2048,416]{0,1:T(8,128)(2,1)S(1)}, bf16[2048,416]{0,1:T(8,128)(2,1)}, u32[]{:S(2)}) copy-start(bf16[2048,416]{0,1:T(8,128)(2,1)} %param.10) | copy-start | bytes 5111812
  43.5 0.9 %copy-start.3 = (s32[64,416]{1,0:T(8,128)S(1)}, s32[64,416]{1,0:T(8,128)}, u32[]{:S(2)}) copy-start(s32[64,416]{1,0:T(8,128)} %up_expo_ref.1) | copy-start | bytes 319492
  56.3 7.5 %collective-permute-start = (f32[128,832]{1,0:T(8,128)S(1)}, f32[128,832]{1,0:T(8,128)S(1)}, u32[]{:S(2)}, u32[]{:S(2)}) collective-permute-start(f32[128,832]{1,0:T(8,128)S(1)} %shard_map.67), channel_id=1, source_target_pairs={{0,128},{128,0},{1,129},{129,1},{2,130},{130,2},{3,131},{131,3},{4... | collective-permute-start | bytes 1277960 | tf_op jit(solution)/shard_map/ppermute | solution.py:100

commit v3 on v2

--- a/solution.py
+++ b/solution.py
@@ -1,3 +1,5 @@
+import itertools
+
 import jax
 import jax.numpy as jnp
 from jax import lax
@@ -10,8 +12,7 @@
 SIZES = (4, 2, 4, 2, 2, 4, 2)
 OUTER = ("yh", "c")
 INNER = ("zh", "zl", "yl", "xh", "xl")
-FAR = ("zh", "xh")
-NEAR = ("zl", "yl", "xl")
+FAR = ("zh", "yl", "xh")
 
 
 def copies_kernel(mant_ref, expo_ref, out_ref):
@@ -32,7 +33,7 @@
     )(mant, expo)
 
 
-def weights_kernel(gate_ref, gate_expo_ref, up_ref, up_expo_ref, out_ref):
+def weights_kernel(gate_ref, gate_expo_ref, up_ref, up_expo_ref, wide_ref, rest_ref):
     def scaled(mant_ref, expo_ref):
         factor = jnp.exp2(expo_ref[...].astype(jnp.float32)).astype(jnp.bfloat16)
         scale = lax.dot_general(
@@ -40,25 +41,41 @@
         )
         return (mant_ref[...].astype(jnp.float32) * scale).astype(jnp.bfloat16)
 
-    blocks, half, width = gate_expo_ref.shape[0], gate_ref.shape[0], gate_ref.shape[1]
-    first = pl.program_id(0) * width
-    block = (first + lax.broadcasted_iota(jnp.int32, (blocks, width), 1)) // 32
+    blocks, width = gate_expo_ref.shape[0], gate_ref.shape[1]
+    step = pl.program_id(0)
+    block = (step * width + lax.broadcasted_iota(jnp.int32, (blocks, width), 1)) // 32
     spread = (block == lax.broadcasted_iota(jnp.int32, (blocks, width), 0)).astype(jnp.bfloat16)
-    out_ref[:half] = scaled(gate_ref, gate_expo_ref)
-    out_ref[half:] = scaled(up_ref, up_expo_ref)
+    both = (scaled(gate_ref, gate_expo_ref), scaled(up_ref, up_expo_ref))
+    turned = jnp.concatenate(both, axis=0).T
+    wide = wide_ref.shape[1]
+    rest = turned.shape[1] - wide
+    wide_ref[...] = turned[:, :wide]
+    for half in range(2):
+
+        @pl.when(step == half)
+        def _():
+            rest_ref[:, half * rest : (half + 1) * rest] = turned[:, wide:]
 
 
 def scaled_weights(gate_mant, gate_expo, up_mant, up_expo):
     depth, half = gate_mant.shape
-    steps = 4
-    mant = pl.BlockSpec((half, depth // steps), lambda i: (0, i))
+    width = depth // 2
+    wide = 2 * half // 128 * 128
+    rest = 2 * half - wide
+    mant = pl.BlockSpec((half, width), lambda i: (0, i))
     expo = pl.BlockSpec(gate_expo.shape, lambda i: (0, 0))
     return pl.pallas_call(
         weights_kernel,
-        grid=(steps,),
+        grid=(2,),
         in_specs=[mant, expo, mant, expo],
-        out_specs=pl.BlockSpec((2 * half, depth // steps), lambda i: (0, i)),
-        out_shape=jax.ShapeDtypeStruct((2 * half, depth), jnp.bfloat16),
+        out_specs=[
+            pl.BlockSpec((width, wide), lambda i: (i, 0)),
+            pl.BlockSpec((width, 2 * rest), lambda i: (0, 0)),
+        ],
+        out_shape=[
+            jax.ShapeDtypeStruct((depth, wide), jnp.bfloat16),
+            jax.ShapeDtypeStruct((width, 2 * rest), jnp.bfloat16),
+        ],
         compiler_params=pltpu.CompilerParams(vmem_limit_bytes=24 << 20),
         cost_estimate=pl.CostEstimate(
             flops=4 * half * depth * 64, bytes_accessed=8 * half * depth, transcendentals=0
@@ -66,16 +83,23 @@
     )(gate_mant.T, gate_expo, up_mant.T, up_expo)
 
 
-def product_kernel(side_ref, rows_ref, weights_ref, out_ref):
+def product_kernel(side_ref, rows_ref, wide_ref, rest_ref, out_ref):
     width = rows_ref.shape[-1]
-    rows = jnp.transpose(rows_ref[0], (2, 0, 3, 1, 4, 5)).reshape(-1, width)
-    out_ref[...] = lax.dot_general(
-        rows, weights_ref[...], (((1,), (1,)), ((), ())), preferred_element_type=jnp.float32
-    )
+    rows = jnp.transpose(rows_ref[0], (1, 2, 3, 0, 4, 5)).reshape(-1, width)
+    wide, rest = wide_ref.shape[1], rest_ref.shape[1] // 2
+
+    def dot(x, y):
+        return jnp.dot(x, y, preferred_element_type=jnp.float32)
+
+    out_ref[:, :wide] = dot(rows, wide_ref[...])
+    lower = dot(rows[:, : width // 2], rest_ref[...])
+    upper = dot(rows[:, width // 2 :], rest_ref[...])
+    out_ref[:, wide:] = lower[:, :rest] + upper[:, rest:]
 
 
 def product(side, everyone, weights):
-    count, units = everyone.size // everyone.shape[-1] // 2, weights.shape[0]
+    wide, rest = weights
+    count, units = everyone.size // everyone.shape[-1] // 2, wide.shape[1] + rest.shape[1] // 2
     return pl.pallas_call(
         product_kernel,
         grid_spec=pltpu.PrefetchScalarGridSpec(
@@ -83,16 +107,17 @@
             grid=(1,),
             in_specs=[
                 pl.BlockSpec((1,) + everyone.shape[1:], lambda i, side: (side[0],) + (0,) * 6),
-                pl.BlockSpec(weights.shape, lambda i, side: (0, 0)),
+                pl.BlockSpec(wide.shape, lambda i, side: (0, 0)),
+                pl.BlockSpec(rest.shape, lambda i, side: (0, 0)),
             ],
             out_specs=pl.BlockSpec((count, units), lambda i, side: (0, 0)),
         ),
         out_shape=jax.ShapeDtypeStruct((count, units), jnp.float32),
         compiler_params=pltpu.CompilerParams(vmem_limit_bytes=24 << 20),
         cost_estimate=pl.CostEstimate(
-            flops=2 * count * weights.size, bytes_accessed=2 * weights.size, transcendentals=0
+            flops=2 * count * wide.size, bytes_accessed=2 * wide.size, transcendentals=0
         ),
-    )(side.reshape(1), everyone, weights)
+    )(side.reshape(1), everyone, wide, rest)
 
 
 def summed_shares(everyone, weights):
@@ -103,10 +128,33 @@
     return jnp.sum(parts, axis=0)
 
 
+def copied_kernel(block_ref, out_ref):
+    out_ref[...] = jnp.broadcast_to(block_ref[...][None], out_ref.shape)
+
+
+def copied(block, count):
+    return pl.pallas_call(
+        copied_kernel,
+        out_shape=jax.ShapeDtypeStruct((count,) + block.shape, block.dtype),
+        compiler_params=pltpu.CompilerParams(vmem_limit_bytes=16 << 20),
+    )(block)
+
+
+def squares():
+    groups = []
+    for outer, a, yl, b in itertools.product(range(8), range(4), range(2), range(4)):
+        core = outer % 2
+        zs = sorted(((2 * a + core) % 8, (2 * a + core + 1) % 8), key=lambda z: z % 2)
+        xs = sorted(((2 * b + core) % 8, (2 * b + core + 1) % 8), key=lambda x: x % 2)
+        groups.append([((outer * 8 + z) * 2 + yl) * 8 + x for z in zs for x in xs])
+    return groups
+
+
 def gathered(tok_mant, tok_expo):
-    far = lax.all_to_all(scaled_copies(tok_mant, tok_expo, 16), FAR, 0, 0)
-    near = lax.all_to_all(jnp.broadcast_to(far[None], (8,) + far.shape), NEAR, 0, 0)
-    return near.reshape((2, 2, 2, 4, 4) + tok_mant.shape)
+    far = lax.all_to_all(scaled_copies(tok_mant, tok_expo, 32), FAR, 0, 0)
+    copies = copied(far, 4)
+    near = lax.all_to_all(copies, AXES, 0, 0, axis_index_groups=squares())
+    return near.reshape((2, 2, 4, 2, 4) + tok_mant.shape)
 
 
 def local(tok_mant, tok_expo, gate_mant, gate_expo, up_mant, up_expo):

time: 85.6 us -> 83.8 us (0.979)
  waiting for transfers between devices: 7.32 us -> 3.85 us
  blocking collectives: 53.4 us -> 56.8 us
  local copies, waits for them, and re-layouts: 5.54 us -> 3.81 us
    all_to_all x1, waiting for transfers between devices: 7.32 us -> 3.85 us  [gathered(): near = lax.all_to_all(copies, AXES, 0, 0, axis_index_groups=squares())]
    all_to_all x1, blocking collectives: 32.9 us -> 36.1 us  [gathered(): far = lax.all_to_all(scaled_copies(tok_mant, tok_expo, 32), FAR, 0, 0)]
    broadcast_in_dim x1 -> x0, local copies, waits for them, and re-layouts: 1.73 us -> none  [gathered(): jnp.broadcast_to(far[None], (8,) + far.shape)]
    pallas_call x2, Pallas kernels: 4.62 us -> 3.65 us  [product(): pl.pallas_call(product_kernel, grid_spec=pltpu.PrefetchScalarGridSpec(num...]
    pallas_call x1 -> x2, Pallas kernels: 2.21 us -> 3.09 us  [the longest x1 1.99 us: scaled_weights(): pl.pallas_call(weights_kernel, grid=(2,), in_specs=[mant, expo, mant, exp...]
where the time goes in v3:
time: 83.8 us; the launch traced here: 83.2 us
  blocking collectives  56.8 us (68%)
  starting transfers between devices  9.6 us (11%)
  Pallas kernels  8.31 us (10%)
  waiting for transfers between devices  3.85 us (5%)
  local copies, waits for them, and re-layouts  3.81 us (5%)
    all_to_all x1, blocking collectives, gathered(): far = lax.all_to_all(scaled_copies(tok_mant, tok_expo, 32), FAR, 0, 0)  36.1 us
    all_to_all x1, blocking collectives, summed_shares(): parts = lax.all_to_all(pair.reshape(4, 32, -1), 'yh', 0, 0)  20.7 us
    ppermute x1, starting transfers between devices, summed_shares(): lax.ppermute(product(1 - core, everyone, weights), 'c', [(0, 1), (1, 0)])  5.36 us
    all_to_all x1, starting transfers between devices, gathered(): near = lax.all_to_all(copies, AXES, 0, 0, axis_index_groups=squares())  4.24 us
    all_to_all x1, waiting for transfers between devices, gathered(): near = lax.all_to_all(copies, AXES, 0, 0, axis_index_groups=squares())  3.85 us
    unnamed x8, local copies, waits for them, and re-layouts  3.81 us
    pallas_call x2, Pallas kernels, product(): pl.pallas_call(product_kernel, grid_spec=pltpu.PrefetchScalarGridSpec(num...  3.65 us
    pallas_call x1, Pallas kernels, scaled_weights(): pl.pallas_call(weights_kernel, grid=(2,), in_specs=[mant, expo, mant, exp...  1.99 us
  transfers between devices with their start and end apart: 2, of which 1 were waited for; matrix products, arithmetic and copies ran while one was open for 0% of the time, Pallas kernels for 5%

profile of v3, /device:TPU:1, one launch (start us, length us, event | category | flops | bytes accessed | tf_op | source)
XLA Modules:
  0.0 83.2 jit_solution(4131531754823623591)
XLA Ops:
  0.0 1.6 %shard_map.64 = bf16[32,2,2048]{2,1,0:T(2,128)(2,1)} custom-call(bf16[2,2048]{1,0:T(2,128)(2,1)} %mant_ref.1, s32[2,64]{1,0:T(2,128)} %expo_ref.1), custom_call_target="tpu_custom_call" | custom-call | tf_op jit(solution)/shard_map/pallas_call | solution.py:29
  1.6 36.1 %all_to_all.15.block_ref = bf16[32,2,2048]{2,1,0:T(2,128)(2,1)S(1)} all-to-all(bf16[32,2,2048]{2,1,0:T(2,128)(2,1)} %shard_map.64), channel_id=1, replica_groups=mesh['yh'=4,'c'=2,'zh'=4,'zl'=2,'yl'=2,'xh'=4,'xl'=2] {'zh','yl','xh'}, dimensions={0} | all-to-all | bytes 524288 | tf_op jit(solution)/shard_map/all_to_all | solution.py:154
  37.7 0.0 copy-start.2
  37.7 1.1 %shard_map.65 = bf16[4,32,2,2048]{3,2,1,0:T(2,128)(2,1)} custom-call(bf16[32,2,2048]{2,1,0:T(2,128)(2,1)S(1)} %all_to_all.15.block_ref), custom_call_target="tpu_custom_call" | custom-call | tf_op jit(solution)/shard_map/pallas_call | solution.py:136
  38.8 4.2 %all-to-all-start.1 = ((bf16[4,32,2,2048]{3,2,1,0:T(2,128)(2,1)}), bf16[4,32,2,2048]{3,2,1,0:T(2,128)(2,1)}, u32[]{:S(2)}, u32[]{:S(2)}) async-start(bf16[4,32,2,2048]{3,2,1,0:T(2,128)(2,1)} %shard_map.65), calls=%async_computation.1 | async-start | bytes 2097152 | tf_op jit(solution)/shard_map/all_to_all | solution.py:156
  43.0 0.0 copy-done.2
  43.0 0.0 copy-start
  43.0 1.4 %copy-done = bf16[2048,416]{0,1:T(8,128)(2,1)S(1)} copy-done((bf16[2048,416]{0,1:T(8,128)(2,1)S(1)}, bf16[2048,416]{0,1:T(8,128)(2,1)}, u32[]{:S(2)}) %copy-start) | copy-done | bytes 1703960
  44.5 0.0 copy-start.1
  44.5 1.5 %copy-done.1 = bf16[2048,416]{0,1:T(8,128)(2,1)S(1)} copy-done((bf16[2048,416]{0,1:T(8,128)(2,1)S(1)}, bf16[2048,416]{0,1:T(8,128)(2,1)}, u32[]{:S(2)}) %copy-start.1) | copy-done | bytes 1703960
  45.9 0.0 copy-start.3
  45.9 0.9 %copy-done.3 = s32[64,416]{1,0:T(8,128)S(1)} copy-done((s32[64,416]{1,0:T(8,128)S(1)}, s32[64,416]{1,0:T(8,128)}, u32[]{:S(2)}) %copy-start.3) | copy-done | bytes 106520
  46.8 2.0 %shard_map.66 = (bf16[2048,768]{1,0:T(8,128)(2,1)S(1)}, bf16[1024,128]{1,0:T(8,128)(2,1)S(1)}) custom-call(bf16[416,2048]{1,0:T(8,128)(2,1)S(1)} %bitcast.6, s32[64,416]{1,0:T(8,128)S(1)} %copy-done.2, bf16[416,2048]{1,0:T(8,128)(2,1)S(1)} %bitcast.7, s32[64,416]{1,0:T(8,128)S(1)} %copy-done.3), custom_call_target="tpu_custom_call" | custom-call | flops 218103808 | bytes 6815744 | tf_op jit(solution)/shard_map/pallas_call | solution.py:67
  48.8 3.9 %all-to-all-done.1 = bf16[4,32,2,2048]{3,2,1,0:T(2,128)(2,1)} async-done(((bf16[4,32,2,2048]{3,2,1,0:T(2,128)(2,1)}), bf16[4,32,2,2048]{3,2,1,0:T(2,128)(2,1)}, u32[]{:S(2)}, u32[]{:S(2)}) %all-to-all-start.1) | async-done | bytes 1048608 | tf_op jit(solution)/shard_map/all_to_all | solution.py:156
  52.7 1.8 %shard_map.68 = f32[128,832]{1,0:T(8,128)S(1)} custom-call(s32[1]{0:T(128)} %bitcast.4.side_ref, bf16[2,2,4,2,4,2,2048]{6,5,4,3,2,1,0:T(2,128)(2,1)} %bitcast.1.rows_ref, bf16[2048,768]{1,0:T(8,128)(2,1)S(1)} %get-tuple-element.7.wide_ref, bf16[1024,128]{1,0:T(8,128)(2,1)S(1)} %get-tuple-element.8.rest_ref), custom_call_target="tpu_custom_call" | custom-call | flops 402653184 | bytes 3145728 | tf_op jit(solution)/shard_map/pallas_call | solution.py:103
  54.5 5.4 %collective-permute-start = (f32[128,832]{1,0:T(8,128)S(1)}, f32[128,832]{1,0:T(8,128)S(1)}, u32[]{:S(2)}, u32[]{:S(2)}) collective-permute-start(f32[128,832]{1,0:T(8,128)S(1)} %shard_map.68), channel_id=1, source_target_pairs={{0,128},{128,0},{1,129},{129,1},{2,130},{130,2},{3,131},{131,3},{4... | collective-permute-start | bytes 1277960 | tf_op jit(solution)/shard_map/ppermute | solution.py:125
  59.9 1.8 %shard_map.67 = f32[128,832]{1,0:T(8,128)S(1)} custom-call(s32[1]{0:T(128)} %bitcast.side_ref, bf16[2,2,4,2,4,2,2048]{6,5,4,3,2,1,0:T(2,128)(2,1)} %bitcast.1.rows_ref, bf16[2048,768]{1,0:T(8,128)(2,1)S(1)} %get-tuple-element.7.wide_ref, bf16[1024,128]{1,0:T(8,128)(2,1)S(1)} %get-tuple-element.8.rest_ref), custom_call_target="tpu_custom_call" | custom-call | flops 402653184 | bytes 3145728 | tf_op jit(solution)/shard_map/pallas_call | solution.py:103
  61.7 0.0 collective-permute-done
  61.7 0.1 add.7
  61.8 20.7 %all_to_all.16 = f32[4,32,832]{2,1,0:T(8,128)S(1)} all-to-all(f32[4,32,832]{2,1,0:T(8,128)S(1)} %bitcast.8), channel_id=1, replica_groups=mesh['yh'=4,'c'=2,'zh'=4,'zl'=2,'yl'=2,'xh'=4,'xl'=2] {'yh'}, dimensions={0} | all-to-all | bytes 851968 | tf_op jit(solution)/shard_map/all_to_all | solution.py:127
  82.5 0.7 fusion
  (1 shorter events, 0.0 us)
Async XLA Ops:
  37.7 5.4 %copy-start.2 = (s32[64,416]{1,0:T(8,128)S(1)}, s32[64,416]{1,0:T(8,128)}, u32[]{:S(2)}) copy-start(s32[64,416]{1,0:T(8,128)} %gate_expo_ref.1) | copy-start | bytes 319492
  38.8 13.9 %all-to-all-start.1 = ((bf16[4,32,2,2048]{3,2,1,0:T(2,128)(2,1)}), bf16[4,32,2,2048]{3,2,1,0:T(2,128)(2,1)}, u32[]{:S(2)}, u32[]{:S(2)}) async-start(bf16[4,32,2,2048]{3,2,1,0:T(2,128)(2,1)} %shard_map.65), calls=%async_computation.1 | async-start | bytes 2097152 | tf_op jit(solution)/shard_map/all_to_all | solution.py:156
  43.0 1.5 %copy-start = (bf16[2048,416]{0,1:T(8,128)(2,1)S(1)}, bf16[2048,416]{0,1:T(8,128)(2,1)}, u32[]{:S(2)}) copy-start(bf16[2048,416]{0,1:T(8,128)(2,1)} %param.8) | copy-start | bytes 5111812
  44.5 1.5 %copy-start.1 = (bf16[2048,416]{0,1:T(8,128)(2,1)S(1)}, bf16[2048,416]{0,1:T(8,128)(2,1)}, u32[]{:S(2)}) copy-start(bf16[2048,416]{0,1:T(8,128)(2,1)} %param.10) | copy-start | bytes 5111812
  45.9 0.9 %copy-start.3 = (s32[64,416]{1,0:T(8,128)S(1)}, s32[64,416]{1,0:T(8,128)}, u32[]{:S(2)}) copy-start(s32[64,416]{1,0:T(8,128)} %up_expo_ref.1) | copy-start | bytes 319492
  54.5 7.2 %collective-permute-start = (f32[128,832]{1,0:T(8,128)S(1)}, f32[128,832]{1,0:T(8,128)S(1)}, u32[]{:S(2)}, u32[]{:S(2)}) collective-permute-start(f32[128,832]{1,0:T(8,128)S(1)} %shard_map.68), channel_id=1, source_target_pairs={{0,128},{128,0},{1,129},{129,1},{2,130},{130,2},{3,131},{131,3},{4... | collective-permute-start | bytes 1277960 | tf_op jit(solution)/shard_map/ppermute | solution.py:125

commit v4 on v3

--- a/solution.py
+++ b/solution.py
@@ -1,3 +1,4 @@
+import functools
 import itertools
 
 import jax
@@ -120,12 +121,55 @@
     )(side.reshape(1), everyone, wide, rest)
 
 
-def summed_shares(everyone, weights):
+def message_kernel(own_ref, theirs_ref, out_ref):
+    units = own_ref.shape[1]
+    pair = own_ref[...] + theirs_ref[...]
+    is_gate = lax.broadcasted_iota(jnp.int32, pair.shape, 1) < units // 2
+    size = jnp.abs(pair)
+
+    def power(values):
+        top = jnp.max(values, axis=1, keepdims=True)
+        return jnp.ceil(jnp.log2(jnp.maximum(top, 2.0**-100)))
+
+    gate_power = power(jnp.where(is_gate, size, 0.0))
+    up_power = power(jnp.where(is_gate, 0.0, size))
+    scale = jnp.where(is_gate, jnp.exp2(15.0 - gate_power), jnp.exp2(15.0 - up_power))
+    coded = jnp.clip(jnp.round(pair * scale), -32767.0, 32767.0)
+    out_ref[:, :units] = coded.astype(jnp.int32).astype(jnp.int16)
+    rows, spare = out_ref.shape[0], out_ref.shape[1] - units
+    first = lax.broadcasted_iota(jnp.int32, (rows, spare), 1) < spare // 2
+    powers = jnp.where(first, gate_power, up_power)
+    out_ref[:, units:] = powers.astype(jnp.int32).astype(jnp.int16)
+
+
+def hidden_kernel(half, parts_ref, out_ref):
+    parts = parts_ref[...].astype(jnp.int32).astype(jnp.float32)
+    spare = (parts.shape[2] - 2 * half) // 2
+
+    def total(first, place):
+        scale = jnp.exp2(parts[:, :, place : place + 1] - 15.0)
+        return jnp.sum(parts[:, :, first : first + half] * scale, axis=0)
+
+    gate, upper = total(0, 2 * half), total(half, 2 * half + spare)
+    out_ref[...] = (jax.nn.silu(gate) * upper).astype(jnp.bfloat16)
+
+
+def hidden_share(everyone, weights):
     core = lax.axis_index("c")
     theirs = lax.ppermute(product(1 - core, everyone, weights), "c", [(0, 1), (1, 0)])
-    pair = product(core, everyone, weights) + theirs
-    parts = lax.all_to_all(pair.reshape(4, 32, -1), "yh", 0, 0)
-    return jnp.sum(parts, axis=0)
+    own = product(core, everyone, weights)
+    count, units = own.shape
+    message = pl.pallas_call(
+        message_kernel,
+        out_shape=jax.ShapeDtypeStruct((count, units + 64), jnp.int16),
+        compiler_params=pltpu.CompilerParams(vmem_limit_bytes=16 << 20),
+    )(own, theirs)
+    parts = lax.all_to_all(message.reshape(4, count // 4, units + 64), "yh", 0, 0)
+    return pl.pallas_call(
+        functools.partial(hidden_kernel, units // 2),
+        out_shape=jax.ShapeDtypeStruct((count // 4, units // 2), jnp.bfloat16),
+        compiler_params=pltpu.CompilerParams(vmem_limit_bytes=16 << 20),
+    )(parts)
 
 
 def copied_kernel(block_ref, out_ref):
@@ -159,10 +203,7 @@
 
 def local(tok_mant, tok_expo, gate_mant, gate_expo, up_mant, up_expo):
     weights = scaled_weights(gate_mant, gate_expo, up_mant, up_expo)
-    half = gate_mant.shape[1]
-    everyone = gathered(tok_mant, tok_expo)
-    summed = summed_shares(everyone, weights)
-    return (jax.nn.silu(summed[:, :half]) * summed[:, half:]).astype(jnp.bfloat16)
+    return hidden_share(gathered(tok_mant, tok_expo), weights)
 
 
 def solution(mesh):

time: 83.8 us -> 79.1 us (0.944)
  blocking collectives: 56.8 us -> 51.3 us
  Pallas kernels: 8.31 us -> 9.36 us
    all_to_all x1, blocking collectives: 20.7 us -> 15.3 us  [hidden_share(): lax.all_to_all(message.reshape(4, count // 4, units + 64), 'yh', 0, 0)]
    pallas_call x0 -> x2, Pallas kernels: none -> 1.04 us  [the longest x1 0.8 us: hidden_share(): pl.pallas_call(functools.partial(hidden_kernel, units // 2), out_shape=ja...]
where the time goes in v4:
time: 79.1 us; the launch traced here: 78 us
  blocking collectives  51.3 us (65%)
  starting transfers between devices  9.61 us (12%)
  Pallas kernels  9.36 us (12%)
  waiting for transfers between devices  3.85 us (5%)
  local copies, waits for them, and re-layouts  3.81 us (5%)
    all_to_all x1, blocking collectives, gathered(): far = lax.all_to_all(scaled_copies(tok_mant, tok_expo, 32), FAR, 0, 0)  36.1 us
    all_to_all x1, blocking collectives, hidden_share(): lax.all_to_all(message.reshape(4, count // 4, units + 64), 'yh', 0, 0)  15.3 us
    ppermute x1, starting transfers between devices, hidden_share(): lax.ppermute(product(1 - core, everyone, weights), 'c', [(0, 1), (1, 0)])  5.37 us
    all_to_all x1, starting transfers between devices, gathered(): near = lax.all_to_all(copies, AXES, 0, 0, axis_index_groups=squares())  4.24 us
    all_to_all x1, waiting for transfers between devices, gathered(): near = lax.all_to_all(copies, AXES, 0, 0, axis_index_groups=squares())  3.85 us
    unnamed x8, local copies, waits for them, and re-layouts  3.81 us
    pallas_call x2, Pallas kernels, product(): pl.pallas_call(product_kernel, grid_spec=pltpu.PrefetchScalarGridSpec(num...  3.65 us
    pallas_call x1, Pallas kernels, scaled_weights(): pl.pallas_call(weights_kernel, grid=(2,), in_specs=[mant, expo, mant, exp...  1.99 us
  transfers between devices with their start and end apart: 2, of which 1 were waited for; matrix products, arithmetic and copies ran while one was open for 0% of the time, Pallas kernels for 5%

profile of v4, /device:TPU:1, one launch (start us, length us, event | category | flops | bytes accessed | tf_op | source)
XLA Modules:
  0.0 78.0 jit_solution(2800461753163516403)
XLA Ops:
  0.0 1.6 %shard_map.64 = bf16[32,2,2048]{2,1,0:T(2,128)(2,1)} custom-call(bf16[2,2048]{1,0:T(2,128)(2,1)} %mant_ref.1, s32[2,64]{1,0:T(2,128)} %expo_ref.1), custom_call_target="tpu_custom_call" | custom-call | tf_op jit(solution)/shard_map/pallas_call | solution.py:30
  1.6 36.1 %all_to_all.15.block_ref = bf16[32,2,2048]{2,1,0:T(2,128)(2,1)S(1)} all-to-all(bf16[32,2,2048]{2,1,0:T(2,128)(2,1)} %shard_map.64), channel_id=1, replica_groups=mesh['yh'=4,'c'=2,'zh'=4,'zl'=2,'yl'=2,'xh'=4,'xl'=2] {'zh','yl','xh'}, dimensions={0} | all-to-all | bytes 524288 | tf_op jit(solution)/shard_map/all_to_all | solution.py:198
  37.7 0.0 copy-start.2
  37.7 1.1 %shard_map.65 = bf16[4,32,2,2048]{3,2,1,0:T(2,128)(2,1)} custom-call(bf16[32,2,2048]{2,1,0:T(2,128)(2,1)S(1)} %all_to_all.15.block_ref), custom_call_target="tpu_custom_call" | custom-call | tf_op jit(solution)/shard_map/pallas_call | solution.py:180
  38.8 4.2 %all-to-all-start.1 = ((bf16[4,32,2,2048]{3,2,1,0:T(2,128)(2,1)}), bf16[4,32,2,2048]{3,2,1,0:T(2,128)(2,1)}, u32[]{:S(2)}, u32[]{:S(2)}) async-start(bf16[4,32,2,2048]{3,2,1,0:T(2,128)(2,1)} %shard_map.65), calls=%async_computation.1 | async-start | bytes 2097152 | tf_op jit(solution)/shard_map/all_to_all | solution.py:200
  43.0 0.0 copy-done.2
  43.0 0.0 copy-start
  43.0 1.4 %copy-done = bf16[2048,416]{0,1:T(8,128)(2,1)S(1)} copy-done((bf16[2048,416]{0,1:T(8,128)(2,1)S(1)}, bf16[2048,416]{0,1:T(8,128)(2,1)}, u32[]{:S(2)}) %copy-start) | copy-done | bytes 1703960
  44.5 0.0 copy-start.1
  44.5 1.5 %copy-done.1 = bf16[2048,416]{0,1:T(8,128)(2,1)S(1)} copy-done((bf16[2048,416]{0,1:T(8,128)(2,1)S(1)}, bf16[2048,416]{0,1:T(8,128)(2,1)}, u32[]{:S(2)}) %copy-start.1) | copy-done | bytes 1703960
  45.9 0.0 copy-start.3
  46.0 0.9 %copy-done.3 = s32[64,416]{1,0:T(8,128)S(1)} copy-done((s32[64,416]{1,0:T(8,128)S(1)}, s32[64,416]{1,0:T(8,128)}, u32[]{:S(2)}) %copy-start.3) | copy-done | bytes 106520
  46.9 2.0 %shard_map.66 = (bf16[2048,768]{1,0:T(8,128)(2,1)S(1)}, bf16[1024,128]{1,0:T(8,128)(2,1)S(1)}) custom-call(bf16[416,2048]{1,0:T(8,128)(2,1)S(1)} %bitcast.6, s32[64,416]{1,0:T(8,128)S(1)} %copy-done.2, bf16[416,2048]{1,0:T(8,128)(2,1)S(1)} %bitcast.7, s32[64,416]{1,0:T(8,128)S(1)} %copy-done.3), custom_call_target="tpu_custom_call" | custom-call | flops 218103808 | bytes 6815744 | tf_op jit(solution)/shard_map/pallas_call | solution.py:68
  48.9 3.9 %all-to-all-done.1 = bf16[4,32,2,2048]{3,2,1,0:T(2,128)(2,1)} async-done(((bf16[4,32,2,2048]{3,2,1,0:T(2,128)(2,1)}), bf16[4,32,2,2048]{3,2,1,0:T(2,128)(2,1)}, u32[]{:S(2)}, u32[]{:S(2)}) %all-to-all-start.1) | async-done | bytes 1048608 | tf_op jit(solution)/shard_map/all_to_all | solution.py:200
  52.7 1.8 %shard_map.68 = f32[128,832]{1,0:T(8,128)S(1)} custom-call(s32[1]{0:T(128)} %bitcast.4.side_ref, bf16[2,2,4,2,4,2,2048]{6,5,4,3,2,1,0:T(2,128)(2,1)} %bitcast.1.rows_ref, bf16[2048,768]{1,0:T(8,128)(2,1)S(1)} %get-tuple-element.7.wide_ref, bf16[1024,128]{1,0:T(8,128)(2,1)S(1)} %get-tuple-element.8.rest_ref), custom_call_target="tpu_custom_call" | custom-call | flops 402653184 | bytes 3145728 | tf_op jit(solution)/shard_map/pallas_call | solution.py:104
  54.5 5.4 %collective-permute-start = (f32[128,832]{1,0:T(8,128)S(1)}, f32[128,832]{1,0:T(8,128)S(1)}, u32[]{:S(2)}, u32[]{:S(2)}) collective-permute-start(f32[128,832]{1,0:T(8,128)S(1)} %shard_map.68), channel_id=1, source_target_pairs={{0,128},{128,0},{1,129},{129,1},{2,130},{130,2},{3,131},{131,3},{4... | collective-permute-start | bytes 1277960 | tf_op jit(solution)/shard_map/ppermute | solution.py:159
  59.9 1.8 %shard_map.67.own_ref = f32[128,832]{1,0:T(8,128)S(1)} custom-call(s32[1]{0:T(128)} %bitcast.side_ref, bf16[2,2,4,2,4,2,2048]{6,5,4,3,2,1,0:T(2,128)(2,1)} %bitcast.1.rows_ref, bf16[2048,768]{1,0:T(8,128)(2,1)S(1)} %get-tuple-element.7.wide_ref, bf16[1024,128]{1,0:T(8,128)(2,1)S(1)} %get-tuple-element.8.rest_ref), custom_call_target="tpu_custom_call" | custom-call | flops 402653184 | bytes 3145728 | tf_op jit(solution)/shard_map/pallas_call | solution.py:104
  61.7 0.0 collective-permute-done.theirs_ref
  61.7 0.2 shard_map.69
  62.0 15.3 %all_to_all.16.parts_ref = s16[4,32,896]{2,1,0:T(8,128)(2,1)S(1)} all-to-all(s16[4,32,896]{2,1,0:T(8,128)(2,1)S(1)} %bitcast.8), channel_id=1, replica_groups=mesh['yh'=4,'c'=2,'zh'=4,'zl'=2,'yl'=2,'xh'=4,'xl'=2] {'yh'}, dimensions={0} | all-to-all | bytes 458752 | tf_op jit(solution)/shard_map/all_to_all | solution.py:167
  77.2 0.8 %shard_map.70 = bf16[32,416]{1,0:T(8,128)(2,1)} custom-call(s16[4,32,896]{2,1,0:T(8,128)(2,1)S(1)} %all_to_all.16.parts_ref), custom_call_target="tpu_custom_call" | custom-call | tf_op jit(solution)/shard_map/pallas_call | solution.py:168
Async XLA Ops:
  37.7 5.4 %copy-start.2 = (s32[64,416]{1,0:T(8,128)S(1)}, s32[64,416]{1,0:T(8,128)}, u32[]{:S(2)}) copy-start(s32[64,416]{1,0:T(8,128)} %gate_expo_ref.1) | copy-start | bytes 319492
  38.8 13.9 %all-to-all-start.1 = ((bf16[4,32,2,2048]{3,2,1,0:T(2,128)(2,1)}), bf16[4,32,2,2048]{3,2,1,0:T(2,128)(2,1)}, u32[]{:S(2)}, u32[]{:S(2)}) async-start(bf16[4,32,2,2048]{3,2,1,0:T(2,128)(2,1)} %shard_map.65), calls=%async_computation.1 | async-start | bytes 2097152 | tf_op jit(solution)/shard_map/all_to_all | solution.py:200
  43.0 1.5 %copy-start = (bf16[2048,416]{0,1:T(8,128)(2,1)S(1)}, bf16[2048,416]{0,1:T(8,128)(2,1)}, u32[]{:S(2)}) copy-start(bf16[2048,416]{0,1:T(8,128)(2,1)} %param.8) | copy-start | bytes 5111812
  44.5 1.5 %copy-start.1 = (bf16[2048,416]{0,1:T(8,128)(2,1)S(1)}, bf16[2048,416]{0,1:T(8,128)(2,1)}, u32[]{:S(2)}) copy-start(bf16[2048,416]{0,1:T(8,128)(2,1)} %param.10) | copy-start | bytes 5111812
  45.9 0.9 %copy-start.3 = (s32[64,416]{1,0:T(8,128)S(1)}, s32[64,416]{1,0:T(8,128)}, u32[]{:S(2)}) copy-start(s32[64,416]{1,0:T(8,128)} %up_expo_ref.1) | copy-start | bytes 319492
  54.5 7.2 %collective-permute-start = (f32[128,832]{1,0:T(8,128)S(1)}, f32[128,832]{1,0:T(8,128)S(1)}, u32[]{:S(2)}, u32[]{:S(2)}) collective-permute-start(f32[128,832]{1,0:T(8,128)S(1)} %shard_map.68), channel_id=1, source_target_pairs={{0,128},{128,0},{1,129},{129,1},{2,130},{130,2},{3,131},{131,3},{4... | collective-permute-start | bytes 1277960 | tf_op jit(solution)/shard_map/ppermute | solution.py:159

commit v5 on v4

--- a/solution.py
+++ b/solution.py
@@ -14,6 +14,7 @@
 OUTER = ("yh", "c")
 INNER = ("zh", "zl", "yl", "xh", "xl")
 FAR = ("zh", "yl", "xh")
+KEPT = 512
 
 
 def copies_kernel(mant_ref, expo_ref, out_ref):
@@ -34,7 +35,7 @@
     )(mant, expo)
 
 
-def weights_kernel(gate_ref, gate_expo_ref, up_ref, up_expo_ref, wide_ref, rest_ref):
+def weights_kernel(gate_ref, gate_expo_ref, up_ref, up_expo_ref, kept_ref, wide_ref, rest_ref):
     def scaled(mant_ref, expo_ref):
         factor = jnp.exp2(expo_ref[...].astype(jnp.float32)).astype(jnp.bfloat16)
         scale = lax.dot_general(
@@ -48,9 +49,11 @@
     spread = (block == lax.broadcasted_iota(jnp.int32, (blocks, width), 0)).astype(jnp.bfloat16)
     both = (scaled(gate_ref, gate_expo_ref), scaled(up_ref, up_expo_ref))
     turned = jnp.concatenate(both, axis=0).T
-    wide = wide_ref.shape[1]
+    kept = kept_ref.shape[1]
+    wide = kept + wide_ref.shape[1]
     rest = turned.shape[1] - wide
-    wide_ref[...] = turned[:, :wide]
+    kept_ref[...] = turned[:, :kept]
+    wide_ref[...] = turned[:, kept:wide]
     for half in range(2):
 
         @pl.when(step == half)
@@ -70,11 +73,13 @@
         grid=(2,),
         in_specs=[mant, expo, mant, expo],
         out_specs=[
-            pl.BlockSpec((width, wide), lambda i: (i, 0)),
+            pl.BlockSpec((width, KEPT), lambda i: (i, 0)),
+            pl.BlockSpec((width, wide - KEPT), lambda i: (i, 0)),
             pl.BlockSpec((width, 2 * rest), lambda i: (0, 0)),
         ],
         out_shape=[
-            jax.ShapeDtypeStruct((depth, wide), jnp.bfloat16),
+            jax.ShapeDtypeStruct((depth, KEPT), jnp.bfloat16),
+            jax.ShapeDtypeStruct((depth, wide - KEPT), jnp.bfloat16),
             jax.ShapeDtypeStruct((width, 2 * rest), jnp.bfloat16),
         ],
         compiler_params=pltpu.CompilerParams(vmem_limit_bytes=24 << 20),
@@ -84,23 +89,26 @@
     )(gate_mant.T, gate_expo, up_mant.T, up_expo)
 
 
-def product_kernel(side_ref, rows_ref, wide_ref, rest_ref, out_ref):
+def product_kernel(side_ref, rows_ref, kept_ref, wide_ref, rest_ref, out_ref):
     width = rows_ref.shape[-1]
     rows = jnp.transpose(rows_ref[0], (1, 2, 3, 0, 4, 5)).reshape(-1, width)
-    wide, rest = wide_ref.shape[1], rest_ref.shape[1] // 2
+    kept, rest = kept_ref.shape[1], rest_ref.shape[1] // 2
+    wide = kept + wide_ref.shape[1]
 
     def dot(x, y):
         return jnp.dot(x, y, preferred_element_type=jnp.float32)
 
-    out_ref[:, :wide] = dot(rows, wide_ref[...])
+    out_ref[:, :kept] = dot(rows, kept_ref[...])
+    out_ref[:, kept:wide] = dot(rows, wide_ref[...])
     lower = dot(rows[:, : width // 2], rest_ref[...])
     upper = dot(rows[:, width // 2 :], rest_ref[...])
     out_ref[:, wide:] = lower[:, :rest] + upper[:, rest:]
 
 
 def product(side, everyone, weights):
-    wide, rest = weights
-    count, units = everyone.size // everyone.shape[-1] // 2, wide.shape[1] + rest.shape[1] // 2
+    kept, wide, rest = weights
+    units = kept.shape[1] + wide.shape[1] + rest.shape[1] // 2
+    count = everyone.size // everyone.shape[-1] // 2
     return pl.pallas_call(
         product_kernel,
         grid_spec=pltpu.PrefetchScalarGridSpec(
@@ -108,6 +116,7 @@
             grid=(1,),
             in_specs=[
                 pl.BlockSpec((1,) + everyone.shape[1:], lambda i, side: (side[0],) + (0,) * 6),
+                pl.BlockSpec(kept.shape, lambda i, side: (0, 0)),
                 pl.BlockSpec(wide.shape, lambda i, side: (0, 0)),
                 pl.BlockSpec(rest.shape, lambda i, side: (0, 0)),
             ],
@@ -116,9 +125,11 @@
         out_shape=jax.ShapeDtypeStruct((count, units), jnp.float32),
         compiler_params=pltpu.CompilerParams(vmem_limit_bytes=24 << 20),
         cost_estimate=pl.CostEstimate(
-            flops=2 * count * wide.size, bytes_accessed=2 * wide.size, transcendentals=0
+            flops=2 * count * units * everyone.shape[-1],
+            bytes_accessed=2 * units * everyone.shape[-1],
+            transcendentals=0,
         ),
-    )(side.reshape(1), everyone, wide, rest)
+    )(side.reshape(1), everyone, kept, wide, rest)
 
 
 def message_kernel(own_ref, theirs_ref, out_ref):

time: 79.1 us -> 78 us (0.986)
  local copies, waits for them, and re-layouts: 3.81 us -> 6.05 us
  Pallas kernels: 9.36 us -> 7.25 us
    unnamed x8 -> x14, local copies, waits for them, and re-layouts: 3.81 us -> 6.05 us
    pallas_call x2, Pallas kernels: 3.65 us -> 1.57 us  [product(): pl.pallas_call(product_kernel, grid_spec=pltpu.PrefetchScalarGridSpec(num...]
    all_to_all x1, waiting for transfers between devices: 3.85 us -> 2.72 us  [gathered(): near = lax.all_to_all(copies, AXES, 0, 0, axis_index_groups=squares())]
  transfers between devices with their start and end apart: 2 -> 2, of which waited for: 1 -> 2; matrix products, arithmetic and copies ran while one was open for 0% -> 0% of each run, Pallas kernels for 5% -> 4%
where the time goes in v5:
time: 78 us; the launch traced here: 76.8 us
  blocking collectives  51.2 us (66%)
  starting transfers between devices  8.88 us (11%)
  Pallas kernels  7.25 us (9%)
  local copies, waits for them, and re-layouts  6.05 us (8%)
  waiting for transfers between devices  3.33 us (4%)
    all_to_all x1, blocking collectives, gathered(): far = lax.all_to_all(scaled_copies(tok_mant, tok_expo, 32), FAR, 0, 0)  36.1 us
    all_to_all x1, blocking collectives, hidden_share(): lax.all_to_all(message.reshape(4, count // 4, units + 64), 'yh', 0, 0)  15.1 us
    unnamed x14, local copies, waits for them, and re-layouts  6.05 us
    ppermute x1, starting transfers between devices, hidden_share(): lax.ppermute(product(1 - core, everyone, weights), 'c', [(0, 1), (1, 0)])  5.36 us
    all_to_all x1, starting transfers between devices, gathered(): near = lax.all_to_all(copies, AXES, 0, 0, axis_index_groups=squares())  3.51 us
    all_to_all x1, waiting for transfers between devices, gathered(): near = lax.all_to_all(copies, AXES, 0, 0, axis_index_groups=squares())  2.72 us
    pallas_call x1, Pallas kernels, scaled_weights(): pl.pallas_call(weights_kernel, grid=(2,), in_specs=[mant, expo, mant, exp...  2.02 us
    pallas_call x1, Pallas kernels, scaled_copies(): pl.pallas_call(copies_kernel, out_shape=jax.ShapeDtypeStruct((count,) + m...  1.59 us
  transfers between devices with their start and end apart: 2, of which 2 were waited for; matrix products, arithmetic and copies ran while one was open for 0% of the time, Pallas kernels for 4%

profile of v5, /device:TPU:1, one launch (start us, length us, event | category | flops | bytes accessed | tf_op | source)
XLA Modules:
  0.0 76.8 jit_solution(7016991261571094554)
XLA Ops:
  0.0 1.6 %shard_map.64 = bf16[32,2,2048]{2,1,0:T(2,128)(2,1)} custom-call(bf16[2,2048]{1,0:T(2,128)(2,1)} %mant_ref.1, s32[2,64]{1,0:T(2,128)} %expo_ref.1), custom_call_target="tpu_custom_call" | custom-call | tf_op jit(solution)/shard_map/pallas_call | solution.py:31
  1.6 36.1 %all_to_all.15.block_ref = bf16[32,2,2048]{2,1,0:T(2,128)(2,1)S(1)} all-to-all(bf16[32,2,2048]{2,1,0:T(2,128)(2,1)} %shard_map.64), channel_id=1, replica_groups=mesh['yh'=4,'c'=2,'zh'=4,'zl'=2,'yl'=2,'xh'=4,'xl'=2] {'zh','yl','xh'}, dimensions={0} | all-to-all | bytes 524288 | tf_op jit(solution)/shard_map/all_to_all | solution.py:209
  37.7 0.0 copy-start.5
  37.7 1.0 %shard_map.65 = bf16[4,32,2,2048]{3,2,1,0:T(2,128)(2,1)} custom-call(bf16[32,2,2048]{2,1,0:T(2,128)(2,1)S(1)} %all_to_all.15.block_ref), custom_call_target="tpu_custom_call" | custom-call | tf_op jit(solution)/shard_map/pallas_call | solution.py:191
  38.7 3.5 %all-to-all-start.1 = ((bf16[4,32,2,2048]{3,2,1,0:T(2,128)(2,1)}), bf16[4,32,2,2048]{3,2,1,0:T(2,128)(2,1)S(1)}, u32[]{:S(2)}, u32[]{:S(2)}) async-start(bf16[4,32,2,2048]{3,2,1,0:T(2,128)(2,1)} %shard_map.65), calls=%async_computation.1 | async-start | bytes 2097152 | tf_op jit(solution)/shard_map/all_to_all | solution.py:211
  42.3 0.0 copy-done.5
  42.3 0.0 copy-start.3
  42.3 1.4 %copy-done.3 = bf16[2048,416]{0,1:T(8,128)(2,1)S(1)} copy-done((bf16[2048,416]{0,1:T(8,128)(2,1)S(1)}, bf16[2048,416]{0,1:T(8,128)(2,1)}, u32[]{:S(2)}) %copy-start.3) | copy-done | bytes 1703960
  43.7 0.0 copy-start.4
  43.7 1.5 %copy-done.4 = bf16[2048,416]{0,1:T(8,128)(2,1)S(1)} copy-done((bf16[2048,416]{0,1:T(8,128)(2,1)S(1)}, bf16[2048,416]{0,1:T(8,128)(2,1)}, u32[]{:S(2)}) %copy-start.4) | copy-done | bytes 1703960
  45.2 0.0 copy-start.6
  45.2 0.9 %copy-done.6 = s32[64,416]{1,0:T(8,128)S(1)} copy-done((s32[64,416]{1,0:T(8,128)S(1)}, s32[64,416]{1,0:T(8,128)}, u32[]{:S(2)}) %copy-start.6) | copy-done | bytes 106520
  46.1 2.0 %shard_map.66 = (bf16[2048,512]{1,0:T(8,128)(2,1)S(1)}, bf16[2048,256]{1,0:T(8,128)(2,1)S(1)}, bf16[1024,128]{1,0:T(8,128)(2,1)S(1)}) custom-call(bf16[416,2048]{1,0:T(8,128)(2,1)S(1)} %bitcast.8, s32[64,416]{1,0:T(8,128)S(1)} %copy-done.5, bf16[416,2048]{1,0:T(8,128)(2,1)S(1)} %bitcast.9, s32[64,416]{1,0:T(8,128)S(1)} %copy-done.6), custom_call_target="tpu_custom_call" | custom-call | flops 218103808 | bytes 6815744 | tf_op jit(solution)/shard_map/pallas_call | solution.py:71
  48.1 0.0 copy-start
  48.1 1.0 %copy-done = bf16[2048,256]{1,0:T(8,128)(2,1)} copy-done((bf16[2048,256]{1,0:T(8,128)(2,1)}, bf16[2048,256]{1,0:T(8,128)(2,1)S(1)}, u32[]{:S(2)}) %copy-start) | copy-done | bytes 1048600
  49.1 2.7 %all-to-all-done.1 = bf16[4,32,2,2048]{3,2,1,0:T(2,128)(2,1)S(1)} async-done(((bf16[4,32,2,2048]{3,2,1,0:T(2,128)(2,1)}), bf16[4,32,2,2048]{3,2,1,0:T(2,128)(2,1)S(1)}, u32[]{:S(2)}, u32[]{:S(2)}) %all-to-all-start.1) | async-done | bytes 1048608 | tf_op jit(solution)/shard_map/all_to_all | solution.py:211
  51.8 0.0 copy-start.1
  51.8 1.2 %copy-done.1 = bf16[2048,256]{1,0:T(8,128)(2,1)S(1)} copy-done((bf16[2048,256]{1,0:T(8,128)(2,1)S(1)}, bf16[2048,256]{1,0:T(8,128)(2,1)}, u32[]{:S(2)}) %copy-start.1) | copy-done | bytes 1048600
  53.1 0.0 copy-start.2
  53.1 0.8 %shard_map.68 = f32[128,832]{1,0:T(8,128)S(1)} custom-call(s32[1]{0:T(128)} %bitcast.4.side_ref, bf16[2,2,4,2,4,2,2048]{6,5,4,3,2,1,0:T(2,128)(2,1)S(1)} %bitcast.6, bf16[2048,512]{1,0:T(8,128)(2,1)S(1)} %get-tuple-element.8.kept_ref, bf16[2048,256]{1,0:T(8,128)(2,1)S(1)} %copy-done.1, bf16[1024,128]{1,0:T(8,128)(2,1)S(1)} %get-tuple-element.10.rest_ref), custom_call_target="tpu_custom_call" | custom-call | flops 436207616 | bytes 3407872 | tf_op jit(solution)/shard_map/pallas_call | solution.py:112
  53.9 5.4 %collective-permute-start = (f32[128,832]{1,0:T(8,128)S(1)}, f32[128,832]{1,0:T(8,128)S(1)}, u32[]{:S(2)}, u32[]{:S(2)}) collective-permute-start(f32[128,832]{1,0:T(8,128)S(1)} %shard_map.68), channel_id=1, source_target_pairs={{0,128},{128,0},{1,129},{129,1},{2,130},{130,2},{3,131},{131,3},{4... | collective-permute-start | bytes 1277960 | tf_op jit(solution)/shard_map/ppermute | solution.py:170
  59.2 0.0 copy-done.2
  59.2 0.8 %shard_map.67.own_ref = f32[128,832]{1,0:T(8,128)S(1)} custom-call(s32[1]{0:T(128)} %bitcast.side_ref, bf16[2,2,4,2,4,2,2048]{6,5,4,3,2,1,0:T(2,128)(2,1)S(1)} %bitcast.7, bf16[2048,512]{1,0:T(8,128)(2,1)S(1)} %get-tuple-element.8.kept_ref, bf16[2048,256]{1,0:T(8,128)(2,1)S(1)} %copy-done.2, bf16[1024,128]{1,0:T(8,128)(2,1)S(1)} %get-tuple-element.10.rest_ref), custom_call_target="tpu_custom_call" | custom-call | flops 436207616 | bytes 3407872 | tf_op jit(solution)/shard_map/pallas_call | solution.py:112
  60.0 0.6 collective-permute-done.theirs_ref
  60.6 0.2 shard_map.69
  60.9 15.1 %all_to_all.16.parts_ref = s16[4,32,896]{2,1,0:T(8,128)(2,1)S(1)} all-to-all(s16[4,32,896]{2,1,0:T(8,128)(2,1)S(1)} %bitcast.10), channel_id=1, replica_groups=mesh['yh'=4,'c'=2,'zh'=4,'zl'=2,'yl'=2,'xh'=4,'xl'=2] {'yh'}, dimensions={0} | all-to-all | bytes 458752 | tf_op jit(solution)/shard_map/all_to_all | solution.py:178
  76.0 0.8 %shard_map.70 = bf16[32,416]{1,0:T(8,128)(2,1)} custom-call(s16[4,32,896]{2,1,0:T(8,128)(2,1)S(1)} %all_to_all.16.parts_ref), custom_call_target="tpu_custom_call" | custom-call | tf_op jit(solution)/shard_map/pallas_call | solution.py:179
Async XLA Ops:
  37.7 4.6 %copy-start.5 = (s32[64,416]{1,0:T(8,128)S(1)}, s32[64,416]{1,0:T(8,128)}, u32[]{:S(2)}) copy-start(s32[64,416]{1,0:T(8,128)} %gate_expo_ref.1) | copy-start | bytes 319492
  38.7 13.1 %all-to-all-start.1 = ((bf16[4,32,2,2048]{3,2,1,0:T(2,128)(2,1)}), bf16[4,32,2,2048]{3,2,1,0:T(2,128)(2,1)S(1)}, u32[]{:S(2)}, u32[]{:S(2)}) async-start(bf16[4,32,2,2048]{3,2,1,0:T(2,128)(2,1)} %shard_map.65), calls=%async_computation.1 | async-start | bytes 2097152 | tf_op jit(solution)/shard_map/all_to_all | solution.py:211
  42.3 1.5 %copy-start.3 = (bf16[2048,416]{0,1:T(8,128)(2,1)S(1)}, bf16[2048,416]{0,1:T(8,128)(2,1)}, u32[]{:S(2)}) copy-start(bf16[2048,416]{0,1:T(8,128)(2,1)} %param.8) | copy-start | bytes 5111812
  43.7 1.5 %copy-start.4 = (bf16[2048,416]{0,1:T(8,128)(2,1)S(1)}, bf16[2048,416]{0,1:T(8,128)(2,1)}, u32[]{:S(2)}) copy-start(bf16[2048,416]{0,1:T(8,128)(2,1)} %param.10) | copy-start | bytes 5111812
  45.2 0.9 %copy-start.6 = (s32[64,416]{1,0:T(8,128)S(1)}, s32[64,416]{1,0:T(8,128)}, u32[]{:S(2)}) copy-start(s32[64,416]{1,0:T(8,128)} %up_expo_ref.1) | copy-start | bytes 319492
  48.1 1.0 %copy-start = (bf16[2048,256]{1,0:T(8,128)(2,1)}, bf16[2048,256]{1,0:T(8,128)(2,1)S(1)}, u32[]{:S(2)}) copy-start(bf16[2048,256]{1,0:T(8,128)(2,1)S(1)} %get-tuple-element.9.wide_ref) | copy-start | bytes 3145732
  51.8 1.2 %copy-start.1 = (bf16[2048,256]{1,0:T(8,128)(2,1)S(1)}, bf16[2048,256]{1,0:T(8,128)(2,1)}, u32[]{:S(2)}) copy-start(bf16[2048,256]{1,0:T(8,128)(2,1)} %copy-done) | copy-start | bytes 3145732
  53.1 6.2 %copy-start.2 = (bf16[2048,256]{1,0:T(8,128)(2,1)S(1)}, bf16[2048,256]{1,0:T(8,128)(2,1)}, u32[]{:S(2)}) copy-start(bf16[2048,256]{1,0:T(8,128)(2,1)} %copy-done) | copy-start | bytes 3145732
  53.9 6.8 %collective-permute-start = (f32[128,832]{1,0:T(8,128)S(1)}, f32[128,832]{1,0:T(8,128)S(1)}, u32[]{:S(2)}, u32[]{:S(2)}) collective-permute-start(f32[128,832]{1,0:T(8,128)S(1)} %shard_map.68), channel_id=1, source_target_pairs={{0,128},{128,0},{1,129},{129,1},{2,130},{130,2},{3,131},{131,3},{4... | collective-permute-start | bytes 1277960 | tf_op jit(solution)/shard_map/ppermute | solution.py:170

commit v6 on v5

--- a/solution.py
+++ b/solution.py
@@ -15,6 +15,7 @@
 INNER = ("zh", "zl", "yl", "xh", "xl")
 FAR = ("zh", "yl", "xh")
 KEPT = 512
+SPARE = 16
 
 
 def copies_kernel(mant_ref, expo_ref, out_ref):
@@ -79,17 +80,21 @@
         ],
         out_shape=[
             jax.ShapeDtypeStruct((depth, KEPT), jnp.bfloat16),
-            jax.ShapeDtypeStruct((depth, wide - KEPT), jnp.bfloat16),
+            jax.ShapeDtypeStruct((SPARE * depth, wide - KEPT), jnp.bfloat16),
             jax.ShapeDtypeStruct((width, 2 * rest), jnp.bfloat16),
         ],
-        compiler_params=pltpu.CompilerParams(vmem_limit_bytes=24 << 20),
+        compiler_params=pltpu.CompilerParams(vmem_limit_bytes=40 << 20),
         cost_estimate=pl.CostEstimate(
             flops=4 * half * depth * 64, bytes_accessed=8 * half * depth, transcendentals=0
         ),
     )(gate_mant.T, gate_expo, up_mant.T, up_expo)
 
 
-def product_kernel(side_ref, rows_ref, kept_ref, wide_ref, rest_ref, out_ref):
+def product_kernel(
+    side_ref, rows_ref, kept_ref, wide_hbm, rest_ref, out_ref, wide_ref, sem
+):
+    fetch = pltpu.make_async_copy(wide_hbm.at[pl.ds(0, wide_ref.shape[0])], wide_ref, sem)
+    fetch.start()
     width = rows_ref.shape[-1]
     rows = jnp.transpose(rows_ref[0], (1, 2, 3, 0, 4, 5)).reshape(-1, width)
     kept, rest = kept_ref.shape[1], rest_ref.shape[1] // 2
@@ -99,10 +104,11 @@
         return jnp.dot(x, y, preferred_element_type=jnp.float32)
 
     out_ref[:, :kept] = dot(rows, kept_ref[...])
-    out_ref[:, kept:wide] = dot(rows, wide_ref[...])
     lower = dot(rows[:, : width // 2], rest_ref[...])
     upper = dot(rows[:, width // 2 :], rest_ref[...])
     out_ref[:, wide:] = lower[:, :rest] + upper[:, rest:]
+    fetch.wait()
+    out_ref[:, kept:wide] = dot(rows, wide_ref[...])
 
 
 def product(side, everyone, weights):
@@ -117,13 +123,17 @@
             in_specs=[
                 pl.BlockSpec((1,) + everyone.shape[1:], lambda i, side: (side[0],) + (0,) * 6),
                 pl.BlockSpec(kept.shape, lambda i, side: (0, 0)),
-                pl.BlockSpec(wide.shape, lambda i, side: (0, 0)),
+                pl.BlockSpec(memory_space=pl.ANY),
                 pl.BlockSpec(rest.shape, lambda i, side: (0, 0)),
             ],
             out_specs=pl.BlockSpec((count, units), lambda i, side: (0, 0)),
+            scratch_shapes=[
+                pltpu.VMEM((kept.shape[0], wide.shape[1]), wide.dtype),
+                pltpu.SemaphoreType.DMA,
+            ],
         ),
         out_shape=jax.ShapeDtypeStruct((count, units), jnp.float32),
-        compiler_params=pltpu.CompilerParams(vmem_limit_bytes=24 << 20),
+        compiler_params=pltpu.CompilerParams(vmem_limit_bytes=50 << 20),
         cost_estimate=pl.CostEstimate(
             flops=2 * count * units * everyone.shape[-1],
             bytes_accessed=2 * units * everyone.shape[-1],

time: 78 us -> 77.9 us (level)
  Pallas kernels: 7.25 us -> 9.79 us
  local copies, waits for them, and re-layouts: 6.05 us -> 3.81 us
    unnamed x14 -> x8, local copies, waits for them, and re-layouts: 6.05 us -> 3.81 us
    pallas_call x2, Pallas kernels: 1.57 us -> 3.32 us  [product(): pl.pallas_call(product_kernel, grid_spec=pltpu.PrefetchScalarGridSpec(num...]
  transfers between devices with their start and end apart: 2 -> 2, of which waited for: 2 -> 1; matrix products, arithmetic and copies ran while one was open for 0% -> 0% of each run, Pallas kernels for 4% -> 6%
where the time goes in v6:
time: 77.9 us; the launch traced here: 76.8 us
  blocking collectives  51.3 us (66%)
  Pallas kernels  9.79 us (13%)
  starting transfers between devices  8.88 us (11%)
  local copies, waits for them, and re-layouts  3.81 us (5%)
  waiting for transfers between devices  2.97 us (4%)
    all_to_all x1, blocking collectives, gathered(): far = lax.all_to_all(scaled_copies(tok_mant, tok_expo, 32), FAR, 0, 0)  36.1 us
    all_to_all x1, blocking collectives, hidden_share(): lax.all_to_all(message.reshape(4, count // 4, units + 64), 'yh', 0, 0)  15.2 us
    ppermute x1, starting transfers between devices, hidden_share(): lax.ppermute(product(1 - core, everyone, weights), 'c', [(0, 1), (1, 0)])  5.37 us
    unnamed x8, local copies, waits for them, and re-layouts  3.81 us
    all_to_all x1, starting transfers between devices, gathered(): near = lax.all_to_all(copies, AXES, 0, 0, axis_index_groups=squares())  3.51 us
    pallas_call x2, Pallas kernels, product(): pl.pallas_call(product_kernel, grid_spec=pltpu.PrefetchScalarGridSpec(num...  3.32 us
    all_to_all x1, waiting for transfers between devices, gathered(): near = lax.all_to_all(copies, AXES, 0, 0, axis_index_groups=squares())  2.97 us
    pallas_call x1, Pallas kernels, scaled_weights(): pl.pallas_call(weights_kernel, grid=(2,), in_specs=[mant, expo, mant, exp...  2.79 us
  transfers between devices with their start and end apart: 2, of which 1 were waited for; matrix products, arithmetic and copies ran while one was open for 0% of the time, Pallas kernels for 6%

profile of v6, /device:TPU:1, one launch (start us, length us, event | category | flops | bytes accessed | tf_op | source)
XLA Modules:
  0.0 76.8 jit_solution(4658741133711513853)
XLA Ops:
  0.0 0.0 copy-start.2
  0.0 1.6 %shard_map.64 = bf16[32,2,2048]{2,1,0:T(2,128)(2,1)} custom-call(bf16[2,2048]{1,0:T(2,128)(2,1)} %mant_ref.1, s32[2,64]{1,0:T(2,128)} %expo_ref.1), custom_call_target="tpu_custom_call" | custom-call | tf_op jit(solution)/shard_map/pallas_call | solution.py:32
  1.6 36.1 %all_to_all.15.block_ref = bf16[32,2,2048]{2,1,0:T(2,128)(2,1)S(1)} all-to-all(bf16[32,2,2048]{2,1,0:T(2,128)(2,1)} %shard_map.64), channel_id=1, replica_groups=mesh['yh'=4,'c'=2,'zh'=4,'zl'=2,'yl'=2,'xh'=4,'xl'=2] {'zh','yl','xh'}, dimensions={0} | all-to-all | bytes 524288 | tf_op jit(solution)/shard_map/all_to_all | solution.py:219
  37.7 1.0 %shard_map.65 = bf16[4,32,2,2048]{3,2,1,0:T(2,128)(2,1)} custom-call(bf16[32,2,2048]{2,1,0:T(2,128)(2,1)S(1)} %all_to_all.15.block_ref), custom_call_target="tpu_custom_call" | custom-call | tf_op jit(solution)/shard_map/pallas_call | solution.py:201
  38.7 3.5 %all-to-all-start.1 = ((bf16[4,32,2,2048]{3,2,1,0:T(2,128)(2,1)}), bf16[4,32,2,2048]{3,2,1,0:T(2,128)(2,1)S(1)}, u32[]{:S(2)}, u32[]{:S(2)}) async-start(bf16[4,32,2,2048]{3,2,1,0:T(2,128)(2,1)} %shard_map.65), calls=%async_computation.1 | async-start | bytes 2097152 | tf_op jit(solution)/shard_map/all_to_all | solution.py:221
  42.3 0.0 copy-done.2
  42.3 0.0 copy-start
  42.3 1.4 %copy-done = bf16[2048,416]{0,1:T(8,128)(2,1)S(1)} copy-done((bf16[2048,416]{0,1:T(8,128)(2,1)S(1)}, bf16[2048,416]{0,1:T(8,128)(2,1)}, u32[]{:S(2)}) %copy-start) | copy-done | bytes 1703960
  43.7 0.0 copy-start.1
  43.7 1.5 %copy-done.1 = bf16[2048,416]{0,1:T(8,128)(2,1)S(1)} copy-done((bf16[2048,416]{0,1:T(8,128)(2,1)S(1)}, bf16[2048,416]{0,1:T(8,128)(2,1)}, u32[]{:S(2)}) %copy-start.1) | copy-done | bytes 1703960
  45.2 0.0 copy-start.3
  45.2 0.9 %copy-done.3 = s32[64,416]{1,0:T(8,128)S(1)} copy-done((s32[64,416]{1,0:T(8,128)S(1)}, s32[64,416]{1,0:T(8,128)}, u32[]{:S(2)}) %copy-start.3) | copy-done | bytes 106520
  46.1 2.8 %shard_map.66 = (bf16[2048,512]{1,0:T(8,128)(2,1)S(1)}, bf16[32768,256]{1,0:T(8,128)(2,1)}, bf16[1024,128]{1,0:T(8,128)(2,1)S(1)}) custom-call(bf16[416,2048]{1,0:T(8,128)(2,1)S(1)} %bitcast.8, s32[64,416]{1,0:T(8,128)S(1)} %copy-done.2, bf16[416,2048]{1,0:T(8,128)(2,1)S(1)} %bitcast.9, s32[64,416]{1,0:T(8,128)S(1)} %copy-done.3), custom_call_target="tpu_custom_call" | custom-call | flops 218103808 | bytes 6815744 | tf_op jit(solution)/shard_map/pallas_call | solution.py:72
  48.9 3.0 %all-to-all-done.1 = bf16[4,32,2,2048]{3,2,1,0:T(2,128)(2,1)S(1)} async-done(((bf16[4,32,2,2048]{3,2,1,0:T(2,128)(2,1)}), bf16[4,32,2,2048]{3,2,1,0:T(2,128)(2,1)S(1)}, u32[]{:S(2)}, u32[]{:S(2)}) %all-to-all-start.1) | async-done | bytes 1048608 | tf_op jit(solution)/shard_map/all_to_all | solution.py:221
  51.9 1.7 %shard_map.68 = f32[128,832]{1,0:T(8,128)S(1)} custom-call(s32[1]{0:T(128)} %bitcast.4.side_ref, bf16[2,2,4,2,4,2,2048]{6,5,4,3,2,1,0:T(2,128)(2,1)S(1)} %bitcast.6, bf16[2048,512]{1,0:T(8,128)(2,1)S(1)} %get-tuple-element.8.kept_ref, bf16[32768,256]{1,0:T(8,128)(2,1)} %get-tuple-element.9.wide_hbm, bf16[1024,128]{1,0:T(8,128)(2,1)S(1)} %get-tuple-element.10.rest_ref), custom_call_target="tpu_custom_call" | custom-call | flops 436207616 | bytes 3407872 | tf_op jit(solution)/shard_map/pallas_call | solution.py:118
  53.5 5.4 %collective-permute-start = (f32[128,832]{1,0:T(8,128)S(1)}, f32[128,832]{1,0:T(8,128)S(1)}, u32[]{:S(2)}, u32[]{:S(2)}) collective-permute-start(f32[128,832]{1,0:T(8,128)S(1)} %shard_map.68), channel_id=1, source_target_pairs={{0,128},{128,0},{1,129},{129,1},{2,130},{130,2},{3,131},{131,3},{4... | collective-permute-start | bytes 1277960 | tf_op jit(solution)/shard_map/ppermute | solution.py:180
  58.9 1.7 %shard_map.67.own_ref = f32[128,832]{1,0:T(8,128)S(1)} custom-call(s32[1]{0:T(128)} %bitcast.side_ref, bf16[2,2,4,2,4,2,2048]{6,5,4,3,2,1,0:T(2,128)(2,1)S(1)} %bitcast.7, bf16[2048,512]{1,0:T(8,128)(2,1)S(1)} %get-tuple-element.8.kept_ref, bf16[32768,256]{1,0:T(8,128)(2,1)} %get-tuple-element.9.wide_hbm, bf16[1024,128]{1,0:T(8,128)(2,1)S(1)} %get-tuple-element.10.rest_ref), custom_call_target="tpu_custom_call" | custom-call | flops 436207616 | bytes 3407872 | tf_op jit(solution)/shard_map/pallas_call | solution.py:118
  60.6 0.0 collective-permute-done.theirs_ref
  60.6 0.2 shard_map.69
  60.8 15.2 %all_to_all.16.parts_ref = s16[4,32,896]{2,1,0:T(8,128)(2,1)S(1)} all-to-all(s16[4,32,896]{2,1,0:T(8,128)(2,1)S(1)} %bitcast.10), channel_id=1, replica_groups=mesh['yh'=4,'c'=2,'zh'=4,'zl'=2,'yl'=2,'xh'=4,'xl'=2] {'yh'}, dimensions={0} | all-to-all | bytes 458752 | tf_op jit(solution)/shard_map/all_to_all | solution.py:188
  76.0 0.8 %shard_map.70 = bf16[32,416]{1,0:T(8,128)(2,1)} custom-call(s16[4,32,896]{2,1,0:T(8,128)(2,1)S(1)} %all_to_all.16.parts_ref), custom_call_target="tpu_custom_call" | custom-call | tf_op jit(solution)/shard_map/pallas_call | solution.py:189
Async XLA Ops:
  0.0 42.3 %copy-start.2 = (s32[64,416]{1,0:T(8,128)S(1)}, s32[64,416]{1,0:T(8,128)}, u32[]{:S(2)}) copy-start(s32[64,416]{1,0:T(8,128)} %gate_expo_ref.1) | copy-start | bytes 319492
  38.7 13.1 %all-to-all-start.1 = ((bf16[4,32,2,2048]{3,2,1,0:T(2,128)(2,1)}), bf16[4,32,2,2048]{3,2,1,0:T(2,128)(2,1)S(1)}, u32[]{:S(2)}, u32[]{:S(2)}) async-start(bf16[4,32,2,2048]{3,2,1,0:T(2,128)(2,1)} %shard_map.65), calls=%async_computation.1 | async-start | bytes 2097152 | tf_op jit(solution)/shard_map/all_to_all | solution.py:221
  42.3 1.5 %copy-start = (bf16[2048,416]{0,1:T(8,128)(2,1)S(1)}, bf16[2048,416]{0,1:T(8,128)(2,1)}, u32[]{:S(2)}) copy-start(bf16[2048,416]{0,1:T(8,128)(2,1)} %param.8) | copy-start | bytes 5111812
  43.7 1.5 %copy-start.1 = (bf16[2048,416]{0,1:T(8,128)(2,1)S(1)}, bf16[2048,416]{0,1:T(8,128)(2,1)}, u32[]{:S(2)}) copy-start(bf16[2048,416]{0,1:T(8,128)(2,1)} %param.10) | copy-start | bytes 5111812
  45.2 0.9 %copy-start.3 = (s32[64,416]{1,0:T(8,128)S(1)}, s32[64,416]{1,0:T(8,128)}, u32[]{:S(2)}) copy-start(s32[64,416]{1,0:T(8,128)} %up_expo_ref.1) | copy-start | bytes 319492
  53.5 7.0 %collective-permute-start = (f32[128,832]{1,0:T(8,128)S(1)}, f32[128,832]{1,0:T(8,128)S(1)}, u32[]{:S(2)}, u32[]{:S(2)}) collective-permute-start(f32[128,832]{1,0:T(8,128)S(1)} %shard_map.68), channel_id=1, source_target_pairs={{0,128},{128,0},{1,129},{129,1},{2,130},{130,2},{3,131},{131,3},{4... | collective-permute-start | bytes 1277960 | tf_op jit(solution)/shard_map/ppermute | solution.py:180
